TPU v7x, 32 devices: a whole 2x2x4 slice. The times are simulated.
32 devices in a mesh: group: 2 (over y), sky: 4 (over z), visit: 2 (over x), band: 2 (over core).
Axes of the slice: x: 2, y: 2, z: 4, core: 2. Of those that a mesh axis runs over, the one named last changes fastest.
Arguments:
- raw_tiles: bfloat16 [16, 32, 128, 128], P(('group', 'visit', 'band'), 'sky'), parts along dimension 0, may hold values from -6 to 6
- pixel_offsets: int32 [16, 32, 2], P(('group', 'visit', 'band'), 'sky'), parts along dimension 0, may hold values from -1 to 1
- shift_entry_index: int32 [16, 32], P(('group', 'visit', 'band'), 'sky'), parts along dimension 0, may hold values from 0 to 15
- shift_table: float32 [16, 2], replicated, may hold values from 0 to 1
- tile_routes: int32 [16, 32], P(('group', 'visit', 'band'), 'sky'), parts along dimension 0, may hold values from 0 to 31, as said below
- bad_pixels: int32 [16, 32, 32], P('group', 'sky'), parts along dimension 0, may hold values from 0 to 16383, as said below
- basis_kernels: bfloat16 [4, 33, 33], replicated, may hold values from -0.5 to 0.5
- basis_choice: int32 [16, 32], P(('group', 'visit', 'band'), 'sky'), parts along dimension 0, may hold values from 0 to 15
- coef_table: float32 [16, 4], replicated, may hold values from -4 to 4
Outputs:
- difference: bfloat16 [16, 512, 1024], P(('group', 'visit', 'band'), 'sky'), parts along dimension 0
There are 2 independent parts, one for each index of `group`. A program takes and returns all parts, laid end to end along the dimension named above; an argument that names none is the same for every part. Nothing has to cross between parts.
Inputs may be any that keep to these rules, and one draw needn't show every extreme that they name: `tile_routes`: for every visit, each of the 32 slab tiles is named by exactly one source tile. Within each aligned block of 2 visits, the source tiles i with one value of i // 8 name at most 5 slab tiles t with one value of t // 8, and exactly 5 for some value. `bad_pixels`: an entry names the pixel at row r and column c of the slab tile as r * 128 + c. For one slab tile, the entries of all visits together are distinct.
All inputs are finite; a program needn't handle non-finite values.
Results may differ from a plain program's by a relative error of at most 0.018.
Values may be sent and summed in bfloat16 or wider, within the bound.
A program may use at most 128 MiB of HBM per device.

v0:
```python
import jax
import jax.numpy as jnp
from jax import lax
from jax.sharding import PartitionSpec as P


def with_halo(block, sides, width):
    for axis, dim in sides:
        count = lax.axis_size(axis)
        forward = [(i, i + 1) for i in range(count - 1)]
        backward = [(target, source) for source, target in forward]
        low = lax.ppermute(
            lax.slice_in_dim(block, block.shape[dim] - width, None, axis=dim), axis, forward
        )
        high = lax.ppermute(lax.slice_in_dim(block, 0, width, axis=dim), axis, backward)
        block = jnp.concatenate([low, block, high], axis=dim)
    return block


def lanczos(offset):
    return jnp.where(jnp.abs(offset) < 3.0, jnp.sinc(offset) * jnp.sinc(offset / 3.0), 0.0)


def tiles_to_image(tiles):
    visit_count, tile_cols, tile_side = (tiles.shape[0], tiles.shape[1], tiles.shape[2])
    return jnp.transpose(tiles, (0, 2, 1, 3)).reshape(visit_count, tile_side, tile_cols * tile_side)


def hit_planes(listed, tile_side):
    indices = jnp.arange(tile_side)
    row_match_count = (listed[..., None, :] // tile_side == indices[:, None]).astype(jnp.bfloat16)
    column_match_count = (listed[..., None, :] % tile_side == indices[:, None]).astype(jnp.bfloat16)
    return jnp.einsum(
        "...am,...bm->...ab",
        row_match_count,
        column_match_count,
        preferred_element_type=jnp.float32,
    )


def warp_tiles(raw_tiles, pixel_offsets, shift_entry_index, shift_table):
    entries = shift_table.shape[0]
    tile_side = raw_tiles.shape[-1]
    selected_entries = (shift_entry_index[..., None] == jnp.arange(entries)).astype(jnp.float32)
    fraction = jnp.sum(selected_entries[..., None] * shift_table, axis=-2)
    shifts = pixel_offsets.astype(jnp.float32) + fraction
    target_positions = jnp.arange(tile_side).astype(jnp.float32)
    spacing = target_positions[:, None] - target_positions[None, :]
    row_weights = lanczos(spacing - shifts[..., 0, None, None]).astype(jnp.bfloat16)
    col_weights = lanczos(spacing - shifts[..., 1, None, None]).astype(jnp.bfloat16)
    halfway = jnp.einsum(
        "vtap,vtpq->vtaq", row_weights, raw_tiles, preferred_element_type=jnp.float32
    ).astype(jnp.bfloat16)
    return jnp.einsum(
        "vtaq,vtbq->vtab", halfway, col_weights, preferred_element_type=jnp.float32
    ).astype(jnp.bfloat16)


def banded_filter(padded, kernels, tile_side, tile_cols):
    kernel_side = kernels.shape[-1]
    window_width = tile_side + kernel_side - 1
    windows = jnp.stack(
        [padded[:, j * tile_side : j * tile_side + window_width] for j in range(tile_cols)]
    )
    offsets = jnp.arange(window_width)[:, None] - jnp.arange(tile_side)[None, :]
    inside = (offsets >= 0) & (offsets < kernel_side)
    bands = jnp.take(kernels, jnp.clip(offsets, 0, kernel_side - 1), axis=2)
    bands = jnp.where(inside[None, None], bands, jnp.zeros_like(bands))

    def one_tile(window):
        shifted = jnp.stack([window[dy : dy + tile_side] for dy in range(kernel_side)], axis=1)
        return jnp.einsum("adx,bdxc->bac", shifted, bands, preferred_element_type=jnp.float32)

    result = lax.map(one_tile, windows)
    basis_count = kernels.shape[0]
    return (
        jnp.transpose(result, (1, 2, 0, 3))
        .reshape(basis_count, tile_side, tile_cols * tile_side)
        .astype(jnp.bfloat16)
    )


def on_device(
    raw_tiles,
    pixel_offsets,
    shift_entry_index,
    shift_table,
    tile_routes,
    bad_pixels,
    basis_kernels,
    basis_choice,
    coef_table,
):
    visit_count, tile_cols, tile_side = (raw_tiles.shape[0], raw_tiles.shape[1], raw_tiles.shape[2])
    tile_area = tile_side * tile_side
    patches = lax.axis_size("sky")
    capacity = (visit_count * tile_cols + patches - 1) // patches + 1
    seat_count = patches * capacity
    warped = warp_tiles(raw_tiles, pixel_offsets, shift_entry_index, shift_table)
    owners = tile_routes // tile_cols
    slot_ids = tile_routes % tile_cols
    before = jnp.arange(tile_cols)[None, :] < jnp.arange(tile_cols)[:, None]
    shared = owners[:, None, :] == owners[:, :, None]
    queue_rank = jnp.sum(shared & before[None], axis=2)
    seat_ids = owners * capacity + queue_rank
    layout = seat_ids[:, None, :] == jnp.arange(seat_count)[None, :, None]
    outgoing = jnp.einsum(
        "vsk,vkx->vsx",
        layout.astype(jnp.bfloat16),
        warped.reshape(visit_count, tile_cols, tile_area),
        preferred_element_type=jnp.float32,
    ).astype(jnp.bfloat16)
    labels = (jnp.sum(jnp.where(layout, slot_ids[:, None, :] + 1, 0), axis=2) - 1).astype(
        jnp.bfloat16
    )
    arrived, arrived_labels = (
        lax.all_to_all(
            outgoing.reshape(visit_count, patches, capacity * tile_area),
            "sky",
            split_axis=1,
            concat_axis=1,
            tiled=True,
        ),
        lax.all_to_all(
            labels.reshape(visit_count, patches, capacity),
            "sky",
            split_axis=1,
            concat_axis=1,
            tiled=True,
        ),
    )
    landing = (
        arrived_labels.astype(jnp.float32).reshape(visit_count, seat_count)[:, None, :]
        == jnp.arange(tile_cols).astype(jnp.float32)[None, :, None]
    )
    placed = jnp.einsum(
        "vks,vsx->vkx",
        landing.astype(jnp.bfloat16),
        arrived.reshape(visit_count, seat_count, tile_area),
        preferred_element_type=jnp.float32,
    ).astype(jnp.bfloat16)
    slab_image = tiles_to_image(placed.reshape(visit_count, tile_cols, tile_side, tile_side))
    shard_index = lax.axis_index(("visit", "band"))
    visit_total = bad_pixels.shape[0]
    listed_count = bad_pixels.shape[2]
    own_listed = lax.dynamic_slice_in_dim(bad_pixels, shard_index * visit_count, visit_count, 0)
    own_flags = tiles_to_image(hit_planes(own_listed, tile_side))
    valid_pixel_mask = 1.0 - own_flags
    all_listed = jnp.transpose(bad_pixels, (1, 0, 2)).reshape(
        1, tile_cols, visit_total * listed_count
    )
    all_flags = tiles_to_image(hit_planes(all_listed, tile_side))[0]
    tallies = visit_total - all_flags
    values = slab_image.astype(jnp.float32)
    partial_sums = jnp.sum(valid_pixel_mask * values, axis=0)
    partial_high = jnp.max(jnp.where(valid_pixel_mask > 0.5, slab_image, -jnp.inf), axis=0)
    partial_low = jnp.min(jnp.where(valid_pixel_mask > 0.5, slab_image, jnp.inf), axis=0)
    summed = lax.psum(partial_sums.astype(jnp.bfloat16), ("visit", "band")).astype(jnp.float32)
    highest = lax.pmax(partial_high, ("visit", "band"))
    lowest = lax.pmin(partial_low, ("visit", "band"))
    coadded = (
        (summed - highest.astype(jnp.float32) - lowest.astype(jnp.float32)) / (tallies - 2.0)
    ).astype(jnp.bfloat16)
    margin = basis_kernels.shape[-1] // 2
    padded = with_halo(coadded, (("sky", 0),), margin)
    padded = jnp.pad(padded, ((0, 0), (margin, margin)))
    per_device = basis_kernels.shape[0] // lax.axis_size("visit")
    own_kernels = lax.dynamic_slice_in_dim(
        basis_kernels, lax.axis_index("visit") * per_device, per_device, 0
    )
    filtered = lax.all_gather(
        banded_filter(padded, own_kernels, tile_side, tile_cols), "visit", axis=0, tiled=True
    )
    entries = coef_table.shape[0]
    picks = (basis_choice[..., None] == jnp.arange(entries)).astype(jnp.float32)
    mixture = jnp.sum(picks[..., None] * coef_table, axis=2)
    basis_count = basis_kernels.shape[0]
    basis_planes = filtered.astype(jnp.float32).reshape(
        basis_count, tile_side, tile_cols, tile_side
    )
    template = jnp.einsum(
        "vkb,bakc->vakc", mixture, basis_planes, precision=lax.Precision.HIGHEST
    ).reshape(visit_count, tile_side, tile_cols * tile_side)
    return ((values - template) * valid_pixel_mask).astype(jnp.bfloat16)


def solution(mesh):
    return jax.shard_map(
        on_device,
        mesh=mesh,
        in_specs=(
            P(("group", "visit", "band"), "sky", None, None),
            P(("group", "visit", "band"), "sky", None),
            P(("group", "visit", "band"), "sky"),
            P(),
            P(("group", "visit", "band"), "sky"),
            P("group", "sky", None),
            P(),
            P(("group", "visit", "band"), "sky"),
            P(),
        ),
        out_specs=P(("group", "visit", "band"), "sky", None),
        check_vma=False,
    )
```

profile of v0, /device:TPU:0, one launch (start us, length us, event | category | flops | bytes accessed | tf_op | source)
XLA Modules:
  0.0 321.6 jit_solution(13471910060581517322)
XLA Ops:
  8.3 6.3 %all-to-all-start = ((bf16[2,4,5]{2,0,1:T(2,128)(2,1)}), bf16[2,4,5]{2,0,1:T(2,128)(2,1)S(1)}, u32[]{:S(2)}, u32[]{:S(2)}) async-start(bf16[2,4,5]{2,0,1:T(2,128)(2,1)} %copy.60), calls=%async_computation | async-start | bytes 4096 | tf_op jit(solution)/shard_map/all_to_all | solution.py:124
  16.9 5.2 %convolution_convert_fusion.2 = bf16[2,8,128,128]{3,2,1,0:T(8,128)(2,1)S(1)} fusion(bf16[2,8,128,128]{3,2,1,0:T(8,128)(2,1)S(1)} %copy-done, f32[2,8]{1,0:T(2,128)S(1)} %bitcast.308, f32[2,8]{1,0:T(2,128)S(1)} %bitcast.307, f32[128,128]{1,0:T(8,128)S(1)} %broadcast_subtract_fusion), kind=kOutput, calls=%fused_computation.124 | convolution fusion | flops 172490752 | bytes 1114240 | tf_op jit(solution)/shard_map/vtaq,vtbq->vtab/dot_general | solution.py:54
  23.0 1.6 reshape.362
  24.6 2.4 copy.62
  27.0 5.2 %all-to-all-start.1 = ((bf16[2,4,81920]{2,0,1:T(2,128)(2,1)}), bf16[2,4,81920]{2,0,1:T(2,128)(2,1)S(1)}, u32[]{:S(2)}, u32[]{:S(2)}) async-start(bf16[2,4,81920]{2,0,1:T(2,128)(2,1)} %copy.62), calls=%async_computation.1 | async-start | bytes 2621440 | tf_op jit(solution)/shard_map/all_to_all | solution.py:117
  32.5 30.5 %all-to-all-done.1 = bf16[2,4,81920]{2,0,1:T(2,128)(2,1)S(1)} async-done(((bf16[2,4,81920]{2,0,1:T(2,128)(2,1)}), bf16[2,4,81920]{2,0,1:T(2,128)(2,1)S(1)}, u32[]{:S(2)}, u32[]{:S(2)}) %all-to-all-start.1) | async-done | bytes 1310752 | tf_op jit(solution)/shard_map/all_to_all | solution.py:117
  63.0 1.0 copy.63
  65.8 1.9 fusion.106
  70.3 1.2 convolution_subtract_fusion.1
  71.7 132.1 %gather_fusion = bf16[20480,2,33]{2,1,0:T(2,128)(2,1)} fusion(bf16[2,33,33]{1,0,2:T(2,128)(2,1)S(1)} %copy.83, s32[20480]{0:T(1024)S(1)} %fusion.144), kind=kCustom, calls=%fused_computation | custom fusion | bytes 5488640 | tf_op jit(solution)/shard_map/jit(_take)/gather | solution.py:67
  203.8 15.1 %copy.78 = bf16[160,128,2,33]{1,0,2,3:T(8,128)(2,1)S(1)} copy(bf16[160,128,2,33]{3,2,1,0:T(2,128)(2,1)} %bitcast.298) | data formatting | bytes 5406720 | tf_op jit(solution)/shard_map/jit(_take)/gather | solution.py:67
  219.1 1.4 fusion.105
  221.4 2.0 collective-permute-start
  223.4 1.3 collective-permute-start.1
  224.7 1.8 select_bitcast_fusion
  226.5 3.5 %copy.68 = bf16[2,33,160,128]{3,2,1,0:T(8,128)(2,1)} copy(bf16[2,33,160,128]{3,2,0,1:T(8,128)(2,1)} %select_bitcast_fusion) | data formatting | bytes 5406720 | tf_op jit(solution)/shard_map/while | solution.py:74
  230.1 2.8 collective-permute-done.1
  232.9 1.3 pad_maximum_fusion
  234.4 48.8 %while.10 = (s32[]{:T(128)}, bf16[8,2,128,128]{2,3,0,1:T(8,128)(2,1)S(1)}, bf16[8,160,160]{1,2,0:T(8,128)(2,1)S(1)}, bf16[2,33,160,128]{3,2,1,0:T(8,128)(2,1)}, ...) while((s32[]{:T(128)}, ...), condition=%wide.region_10.12_spmd, body=%wide.region_9.11_spmd.sunk | while | flops 346030112 | bytes 7087053 | solution.py:74
  237.9 2.4 fusion.211
  244.0 2.4 fusion.211
  250.0 2.4 fusion.211
  256.1 2.4 fusion.211
  262.2 2.4 fusion.211
  268.3 2.4 fusion.211
  274.4 2.4 fusion.211
  280.5 2.4 fusion.211
  284.5 20.7 %all-gather.2.cloned.1.call-done = bf16[4,128,1024]{2,1,0:T(8,128)(2,1)} async-done(((bf16[2,128,1024]{2,1,0:T(8,128)(2,1)}), bf16[4,128,1024]{2,1,0:T(8,128)(2,1)}) %all-gather.2.cloned.1.call-update) | async-done | bytes 1048592 | tf_op jit(solution)/shard_map/all_gather | solution.py:171
  305.2 1.6 copy.71
  307.6 2.8 fusion.199
  310.3 1.6 copy.74
  313.0 2.0 copy.75
  (359 shorter events, 42.2 us)
Async XLA Ops:
  6.5 10.4 %copy-start = (bf16[2,8,128,128]{3,2,1,0:T(8,128)(2,1)S(1)}, bf16[2,8,128,128]{3,2,1,0:T(8,128)(2,1)}, u32[]{:S(2)}) copy-start(bf16[2,8,128,128]{3,2,1,0:T(8,128)(2,1)} %param.12) | copy-start | bytes 1572868
  8.3 18.7 %all-to-all-start = ((bf16[2,4,5]{2,0,1:T(2,128)(2,1)}), bf16[2,4,5]{2,0,1:T(2,128)(2,1)S(1)}, u32[]{:S(2)}, u32[]{:S(2)}) async-start(bf16[2,4,5]{2,0,1:T(2,128)(2,1)} %copy.60), calls=%async_computation | async-start | bytes 4096 | tf_op jit(solution)/shard_map/all_to_all | solution.py:124
  27.0 5.2 %copy-start.5 = (s32[8,8,32]{2,1,0:T(8,128)S(1)}, s32[8,8,32]{2,1,0:T(8,128)}, u32[]{:S(2)}) copy-start(s32[8,8,32]{2,1,0:T(8,128)} %param.17) | copy-start | bytes 24580
  27.0 36.0 %all-to-all-start.1 = ((bf16[2,4,81920]{2,0,1:T(2,128)(2,1)}), bf16[2,4,81920]{2,0,1:T(2,128)(2,1)S(1)}, u32[]{:S(2)}, u32[]{:S(2)}) async-start(bf16[2,4,81920]{2,0,1:T(2,128)(2,1)} %copy.62), calls=%async_computation.1 | async-start | bytes 2621440 | tf_op jit(solution)/shard_map/all_to_all | solution.py:117
  32.2 186.8 %all-reduce.5.cloned.1.call-start = ((), (), s32[]{:S(2)}) async-start(), calls=%async_computation.2 | async-start | bytes 524288 | tf_op jit(solution)/shard_map/psum | solution.py:158
  65.8 3.7 %copy-start.1 = (bf16[2,8,128,128]{2,3,1,0:T(8,128)(2,1)}, bf16[2,8,128,128]{2,3,1,0:T(8,128)(2,1)S(1)}, u32[]{:S(2)}) copy-start(bf16[2,8,128,128]{2,3,1,0:T(8,128)(2,1)S(1)} %copy.64) | copy-start | bytes 1572868
  67.6 1.0 copy-start.3
  69.5 2.1 copy-start.6
  69.5 149.6 %all-reduce.7.cloned.1.call-start = ((), (), s32[]{:S(2)}) async-start(), calls=%async_computation.3 | async-start | bytes 524288 | tf_op jit(solution)/shard_map/pmax | solution.py:159
  70.2 148.9 %all-reduce.9.cloned.1.call-start = ((), (), s32[]{:S(2)}) async-start(), calls=%async_computation.4 | async-start | bytes 524288 | tf_op jit(solution)/shard_map/pmin | solution.py:160
  71.5 233.7 %all-gather.2.cloned.1.call-start = ((), (), s32[]{:S(2)}) async-start(), calls=%async_computation.5 | async-start | bytes 1572864 | tf_op jit(solution)/shard_map/all_gather | solution.py:171
  221.4 8.6 %collective-permute-start = (bf16[16,1024]{0,1:T(8,128)(2,1)}, bf16[16,1024]{0,1:T(8,128)(2,1)}, u32[]{:S(2)}, u32[]{:S(2)}) collective-permute-start(bf16[16,1024]{0,1:T(8,128)(2,1)} %get-tuple-element.57), channel_id=1, source_target_pairs={{0,4},{4,8},{8,12},{1,5},{5,9},{9,13},{2,6},{6,10},{10,14},{3,7},{... | collective-permute-start | bytes 98312 | tf_op jit(solution)/shard_map/ppermute | solution.py:12
  223.4 9.5 %collective-permute-start.1 = (bf16[16,1024]{0,1:T(8,128)(2,1)}, bf16[16,1024]{0,1:T(8,128)(2,1)}, u32[]{:S(2)}, u32[]{:S(2)}) collective-permute-start(bf16[16,1024]{0,1:T(8,128)(2,1)} %get-tuple-element.58), channel_id=1, source_target_pairs={{4,0},{8,4},{12,8},{5,1},{9,5},{13,9},{6,2},{10,6},{14,10},{7,3},{... | collective-permute-start | bytes 98312 | tf_op jit(solution)/shard_map/ppermute | solution.py:15
  283.1 1.1 copy-start.8
  283.1 1.1 copy-start.7
  310.3 1.6 copy-start.2
  310.3 1.7 copy-start.4
Sparse Core Ops, SparseCore 0:
  69.6 31.0 all-reduce.4
  103.2 32.1 all-reduce.6
  137.8 32.1 all-reduce.8
  284.3 20.8 all-gather.1
where the time goes:
time: 323 us; the launch traced here: 322 us
  local copies, waits for them, and re-layouts  196 us (61%)
  waiting for transfers between devices  54.8 us (17%)
  matrix products  31.6 us (10%)
  starting transfers between devices  14.9 us (5%)
  between operations  13.5 us (4%)
  other arithmetic  10 us (3%)
    gather x2, local copies, waits for them, and re-layouts, banded_filter(): bands = jnp.take(kernels, jnp.clip(offsets, 0, kernel_side - 1), axis=2)  147 us
    all_to_all x1, waiting for transfers between devices, on_device(): lax.all_to_all(outgoing.reshape(visit_count, patches, capacity * tile_are...  30.5 us
    while x256, local copies, waits for them, and re-layouts  26.3 us
    all_gather x1, waiting for transfers between devices, on_device(): lax.all_gather(banded_filter(padded, own_kernels, tile_side, tile_cols),...  20.7 us
    dot_general x8, matrix products, one_tile(): jnp.einsum('adx,bdxc->bac', shifted, bands, preferred_element_type=jnp.fl...  19.5 us
  transfers between devices with their start and end apart: 8, of which 3 were waited for; matrix products, arithmetic and copies ran while one was open for 52% of the time, Pallas kernels for 0%

commit v1 on v0

--- a/solution.py
+++ b/solution.py
@@ -62,14 +62,16 @@
     windows = jnp.stack(
         [padded[:, j * tile_side : j * tile_side + window_width] for j in range(tile_cols)]
     )
-    offsets = jnp.arange(window_width)[:, None] - jnp.arange(tile_side)[None, :]
-    inside = (offsets >= 0) & (offsets < kernel_side)
-    bands = jnp.take(kernels, jnp.clip(offsets, 0, kernel_side - 1), axis=2)
-    bands = jnp.where(inside[None, None], bands, jnp.zeros_like(bands))
+    lead = kernels.shape[:2]
+    padded_rows = jnp.pad(kernels, ((0, 0), (0, 0), (0, window_width + 1 - kernel_side)))
+    repeated = jnp.broadcast_to(
+        padded_rows[:, :, None, :], lead + (tile_side, window_width + 1)
+    ).reshape(lead + (tile_side * (window_width + 1),))
+    bands = repeated[:, :, : tile_side * window_width].reshape(lead + (tile_side, window_width))
 
     def one_tile(window):
         shifted = jnp.stack([window[dy : dy + tile_side] for dy in range(kernel_side)], axis=1)
-        return jnp.einsum("adx,bdxc->bac", shifted, bands, preferred_element_type=jnp.float32)
+        return jnp.einsum("adx,bdcx->bac", shifted, bands, preferred_element_type=jnp.float32)
 
     result = lax.map(one_tile, windows)
     basis_count = kernels.shape[0]

time: 323 us -> 303 us (0.938)
  local copies, waits for them, and re-layouts: 196 us -> 78.8 us
  waiting for transfers between devices: 54.8 us -> 153 us
    gather x2 -> x0, local copies, waits for them, and re-layouts: 147 us -> none  [banded_filter(): bands = jnp.take(kernels, jnp.clip(offsets, 0, kernel_side - 1), axis=2)]
    pmax x1, waiting for transfers between devices: 0.02 us -> 34.6 us  [on_device(): highest = lax.pmax(partial_high, ('visit', 'band'))]
    pmin x1, waiting for transfers between devices: 0.02 us -> 34.6 us  [on_device(): lowest = lax.pmin(partial_low, ('visit', 'band'))]
    psum x1, waiting for transfers between devices: 0.02 us -> 29.3 us  [on_device(): lax.psum(partial_sums.astype(jnp.bfloat16), ('visit', 'band'))]
    reshape x0 -> x2, local copies, waits for them, and re-layouts: none -> 20.5 us  [the longest x1 11.3 us: banded_filter(): repeated = jnp.broadcast_to(padded_rows[:, :, None, :], lead + (tile_side...]
    slice x0 -> x1, local copies, waits for them, and re-layouts: none -> 4.38 us  [banded_filter(): repeated[:, :, :tile_side * window_width]]
  transfers between devices with their start and end apart: 8 -> 8, of which waited for: 3 -> 5; matrix products, arithmetic and copies ran while one was open for 52% -> 15% of each run, Pallas kernels for 0% -> 0%
where the time goes in v1:
time: 303 us; the launch traced here: 302 us
  waiting for transfers between devices  153 us (50%)
  local copies, waits for them, and re-layouts  78.8 us (26%)
  matrix products  30.8 us (10%)
  starting transfers between devices  17 us (6%)
  between operations  13.5 us (4%)
  other arithmetic  7.95 us (3%)
    pmax x1, waiting for transfers between devices, on_device(): highest = lax.pmax(partial_high, ('visit', 'band'))  34.6 us
    pmin x1, waiting for transfers between devices, on_device(): lowest = lax.pmin(partial_low, ('visit', 'band'))  34.6 us
    all_to_all x1, waiting for transfers between devices, on_device(): lax.all_to_all(outgoing.reshape(visit_count, patches, capacity * tile_are...  30.6 us
    psum x1, waiting for transfers between devices, on_device(): lax.psum(partial_sums.astype(jnp.bfloat16), ('visit', 'band'))  29.3 us
    while x256, local copies, waits for them, and re-layouts  26.3 us
    all_gather x1, waiting for transfers between devices, on_device(): lax.all_gather(banded_filter(padded, own_kernels, tile_side, tile_cols),...  22.4 us
    dot_general x8, matrix products, one_tile(): jnp.einsum('adx,bdcx->bac', shifted, bands, preferred_element_type=jnp.fl...  19.5 us
    reshape x1, local copies, waits for them, and re-layouts, banded_filter(): repeated = jnp.broadcast_to(padded_rows[:, :, None, :], lead + (tile_side...  11.3 us
  transfers between devices with their start and end apart: 8, of which 5 were waited for; matrix products, arithmetic and copies ran while one was open for 15% of the time, Pallas kernels for 0%

profile of v1, /device:TPU:0, one launch (start us, length us, event | category | flops | bytes accessed | tf_op | source)
XLA Modules:
  0.0 301.8 jit_solution(5773959515103021066)
XLA Ops:
  8.3 6.3 %all-to-all-start = ((bf16[2,4,5]{2,0,1:T(2,128)(2,1)}), bf16[2,4,5]{2,0,1:T(2,128)(2,1)S(1)}, u32[]{:S(2)}, u32[]{:S(2)}) async-start(bf16[2,4,5]{2,0,1:T(2,128)(2,1)} %copy.54), calls=%async_computation | async-start | bytes 4096 | tf_op jit(solution)/shard_map/all_to_all | solution.py:126
  16.9 5.2 %convolution_convert_fusion.2 = bf16[2,8,128,128]{3,2,1,0:T(8,128)(2,1)S(1)} fusion(bf16[2,8,128,128]{3,2,1,0:T(8,128)(2,1)S(1)} %copy-done, f32[2,8]{1,0:T(2,128)S(1)} %bitcast.306, f32[2,8]{1,0:T(2,128)S(1)} %bitcast.305, f32[128,128]{1,0:T(8,128)S(1)} %broadcast_subtract_fusion), kind=kOutput, calls=%fused_computation.122 | convolution fusion | flops 172490752 | bytes 1114240 | tf_op jit(solution)/shard_map/vtaq,vtbq->vtab/dot_general | solution.py:54
  23.0 1.6 reshape.312
  24.6 2.4 copy.56
  27.0 5.2 %all-to-all-start.1 = ((bf16[2,4,81920]{2,0,1:T(2,128)(2,1)}), bf16[2,4,81920]{2,0,1:T(2,128)(2,1)S(1)}, u32[]{:S(2)}, u32[]{:S(2)}) async-start(bf16[2,4,81920]{2,0,1:T(2,128)(2,1)} %copy.56), calls=%async_computation.1 | async-start | bytes 2621440 | tf_op jit(solution)/shard_map/all_to_all | solution.py:119
  32.4 30.6 %all-to-all-done.1 = bf16[2,4,81920]{2,0,1:T(2,128)(2,1)S(1)} async-done(((bf16[2,4,81920]{2,0,1:T(2,128)(2,1)}), bf16[2,4,81920]{2,0,1:T(2,128)(2,1)S(1)}, u32[]{:S(2)}, u32[]{:S(2)}) %all-to-all-start.1) | async-done | bytes 1310752 | tf_op jit(solution)/shard_map/all_to_all | solution.py:119
  65.8 1.9 fusion.106
  71.4 29.3 %all-reduce.6.cloned.1.call-done = bf16[128,1024]{0,1:T(8,128)(2,1)} async-done(((bf16[128,1024]{0,1:T(8,128)(2,1)}), bf16[128,1024]{0,1:T(8,128)(2,1)}) %all-reduce.6.cloned.1.call-update) | async-done | bytes 262160 | tf_op jit(solution)/shard_map/psum | solution.py:160
  100.7 34.6 %all-reduce.10.cloned.1.call-done = bf16[128,1024]{0,1:T(8,128)(2,1)} async-done(((bf16[128,1024]{0,1:T(8,128)(2,1)}), bf16[128,1024]{0,1:T(8,128)(2,1)}) %all-reduce.10.cloned.1.call-update) | async-done | bytes 262160 | tf_op jit(solution)/shard_map/pmin | solution.py:162
  135.3 34.6 %all-reduce.8.cloned.1.call-done = bf16[128,1024]{0,1:T(8,128)(2,1)} async-done(((bf16[128,1024]{0,1:T(8,128)(2,1)}), bf16[128,1024]{0,1:T(8,128)(2,1)}) %all-reduce.8.cloned.1.call-update) | async-done | bytes 262160 | tf_op jit(solution)/shard_map/pmax | solution.py:161
  172.1 4.1 %collective-permute-start = (bf16[16,1024]{0,1:T(8,128)(2,1)}, bf16[16,1024]{0,1:T(8,128)(2,1)}, u32[]{:S(2)}, u32[]{:S(2)}) collective-permute-start(bf16[16,1024]{0,1:T(8,128)(2,1)} %get-tuple-element.57), channel_id=1, source_target_pairs={{0,4},{4,8},{8,12},{1,5},{5,9},{9,13},{2,6},{6,10},{10,14},{3,7},{... | collective-permute-start | bytes 98312 | tf_op jit(solution)/shard_map/ppermute | solution.py:12
  176.2 1.3 collective-permute-start.1
  177.6 2.3 broadcast_in_dim.41
  179.8 11.3 %reshape.315 = bf16[2,33,20608]{2,0,1:T(2,128)(2,1)S(1)} reshape(bf16[2,33,128,161]{3,2,0,1:T(8,128)(2,1)} %broadcast_in_dim.41) | data formatting | bytes 5440512 | tf_op jit(solution)/shard_map/reshape | solution.py:69
  191.1 4.4 %slice.200 = bf16[2,33,20480]{2,0,1:T(2,128)(2,1)} slice(bf16[2,33,20608]{2,0,1:T(2,128)(2,1)S(1)} %reshape.315), slice={[0:2], [0:33], [0:20480]} | slice | bytes 5406720 | tf_op jit(solution)/shard_map/slice | solution.py:70
  195.5 9.3 %reshape.316 = bf16[2,33,128,160]{3,2,0,1:T(8,128)(2,1)} reshape(bf16[2,33,20480]{2,0,1:T(2,128)(2,1)} %slice.200) | data formatting | bytes 5406720 | tf_op jit(solution)/shard_map/reshape | solution.py:70
  204.8 5.8 %copy.60 = bf16[2,33,128,160]{2,3,1,0:T(8,128)(2,1)} copy(bf16[2,33,128,160]{3,2,0,1:T(8,128)(2,1)} %reshape.316) | data formatting | bytes 5406720 | tf_op jit(solution)/shard_map/while | solution.py:76
  210.6 1.3 pad_maximum_fusion
  213.0 48.7 %while.10 = (s32[]{:T(128)}, bf16[8,2,128,128]{2,3,0,1:T(8,128)(2,1)S(1)}, bf16[8,160,160]{1,2,0:T(8,128)(2,1)S(1)}, bf16[2,33,128,160]{2,3,1,0:T(8,128)(2,1)}, ...) while((s32[]{:T(128)}, ...), condition=%wide.region_10.12_spmd, body=%wide.region_9.11_spmd.sunk | while | flops 346030112 | bytes 7087053 | solution.py:76
  216.5 2.4 fusion.203
  222.6 2.4 fusion.203
  228.7 2.4 fusion.203
  234.8 2.4 fusion.203
  240.9 2.4 fusion.203
  246.9 2.4 fusion.203
  253.0 2.4 fusion.203
  259.1 2.4 fusion.203
  263.1 22.4 %all-gather.2.cloned.1.call-done = bf16[4,128,1024]{2,1,0:T(8,128)(2,1)} async-done(((bf16[2,128,1024]{2,1,0:T(8,128)(2,1)}), bf16[4,128,1024]{2,1,0:T(8,128)(2,1)}) %all-gather.2.cloned.1.call-update) | async-done | bytes 1048592 | tf_op jit(solution)/shard_map/all_gather | solution.py:173
  285.4 1.6 copy.63
  287.8 2.8 fusion.191
  290.6 1.6 copy.66
  293.2 2.0 copy.67
  (360 shorter events, 46.1 us)
Async XLA Ops:
  6.5 10.4 %copy-start = (bf16[2,8,128,128]{3,2,1,0:T(8,128)(2,1)S(1)}, bf16[2,8,128,128]{3,2,1,0:T(8,128)(2,1)}, u32[]{:S(2)}) copy-start(bf16[2,8,128,128]{3,2,1,0:T(8,128)(2,1)} %param.12) | copy-start | bytes 1572868
  8.3 18.7 %all-to-all-start = ((bf16[2,4,5]{2,0,1:T(2,128)(2,1)}), bf16[2,4,5]{2,0,1:T(2,128)(2,1)S(1)}, u32[]{:S(2)}, u32[]{:S(2)}) async-start(bf16[2,4,5]{2,0,1:T(2,128)(2,1)} %copy.54), calls=%async_computation | async-start | bytes 4096 | tf_op jit(solution)/shard_map/all_to_all | solution.py:126
  27.0 5.2 %copy-start.6 = (s32[8,8,32]{2,1,0:T(8,128)S(1)}, s32[8,8,32]{2,1,0:T(8,128)}, u32[]{:S(2)}) copy-start(s32[8,8,32]{2,1,0:T(8,128)} %param.17) | copy-start | bytes 24580
  27.0 36.0 %all-to-all-start.1 = ((bf16[2,4,81920]{2,0,1:T(2,128)(2,1)}), bf16[2,4,81920]{2,0,1:T(2,128)(2,1)S(1)}, u32[]{:S(2)}, u32[]{:S(2)}) async-start(bf16[2,4,81920]{2,0,1:T(2,128)(2,1)} %copy.56), calls=%async_computation.1 | async-start | bytes 2621440 | tf_op jit(solution)/shard_map/all_to_all | solution.py:119
  32.2 68.5 %all-reduce.6.cloned.1.call-start = ((), (), s32[]{:S(2)}) async-start(), calls=%async_computation.2 | async-start | bytes 524288 | tf_op jit(solution)/shard_map/psum | solution.py:160
  65.8 3.7 %copy-start.1 = (bf16[2,8,128,128]{2,3,1,0:T(8,128)(2,1)}, bf16[2,8,128,128]{2,3,1,0:T(8,128)(2,1)S(1)}, u32[]{:S(2)}) copy-start(bf16[2,8,128,128]{2,3,1,0:T(8,128)(2,1)S(1)} %copy.58) | copy-start | bytes 1572868
  67.6 1.0 copy-start.3
  69.5 65.8 %all-reduce.10.cloned.1.call-start = ((), (), s32[]{:S(2)}) async-start(), calls=%async_computation.4 | async-start | bytes 524288 | tf_op jit(solution)/shard_map/pmin | solution.py:162
  70.2 99.7 %all-reduce.8.cloned.1.call-start = ((), (), s32[]{:S(2)}) async-start(), calls=%async_computation.3 | async-start | bytes 524288 | tf_op jit(solution)/shard_map/pmax | solution.py:161
  70.9 214.5 %all-gather.2.cloned.1.call-start = ((), (), s32[]{:S(2)}) async-start(), calls=%async_computation.5 | async-start | bytes 1572864 | tf_op jit(solution)/shard_map/all_gather | solution.py:173
  71.4 106.1 %copy-start.7 = (bf16[4,33,33]{2,0,1:T(4,128)(2,1)S(1)}, bf16[4,33,33]{2,0,1:T(4,128)(2,1)}, u32[]{:S(2)}) copy-start(bf16[4,33,33]{2,0,1:T(4,128)(2,1)} %param.18) | copy-start | bytes 26140
  172.1 38.5 %collective-permute-start = (bf16[16,1024]{0,1:T(8,128)(2,1)}, bf16[16,1024]{0,1:T(8,128)(2,1)}, u32[]{:S(2)}, u32[]{:S(2)}) collective-permute-start(bf16[16,1024]{0,1:T(8,128)(2,1)} %get-tuple-element.57), channel_id=1, source_target_pairs={{0,4},{4,8},{8,12},{1,5},{5,9},{9,13},{2,6},{6,10},{10,14},{3,7},{... | collective-permute-start | bytes 98312 | tf_op jit(solution)/shard_map/ppermute | solution.py:12
  176.2 34.4 %collective-permute-start.1 = (bf16[16,1024]{0,1:T(8,128)(2,1)}, bf16[16,1024]{0,1:T(8,128)(2,1)}, u32[]{:S(2)}, u32[]{:S(2)}) collective-permute-start(bf16[16,1024]{0,1:T(8,128)(2,1)} %get-tuple-element.58), channel_id=1, source_target_pairs={{4,0},{8,4},{12,8},{5,1},{9,5},{13,9},{6,2},{10,6},{14,10},{7,3},{... | collective-permute-start | bytes 98312 | tf_op jit(solution)/shard_map/ppermute | solution.py:15
  212.0 1.0 copy-start.5
  261.7 1.1 copy-start.9
  261.7 1.1 copy-start.8
  290.6 1.6 copy-start.2
  290.6 1.7 copy-start.4
Sparse Core Ops, SparseCore 0:
  69.6 31.0 all-reduce.5
  103.1 32.1 all-reduce.9
  137.8 32.1 all-reduce.7
  262.9 22.4 all-gather.1

commit v2 on v0

v2 whole, which is shorter than its diff:
```python
import functools

import jax
import jax.numpy as jnp
from jax import lax
from jax.experimental import pallas as pl
from jax.experimental.pallas import tpu as pltpu
from jax.sharding import PartitionSpec as P


def lanczos(offset):
    return jnp.where(jnp.abs(offset) < 3.0, jnp.sinc(offset) * jnp.sinc(offset / 3.0), 0.0)


def hit_planes(listed, tile_side):
    indices = jnp.arange(tile_side)
    row_match_count = (listed[..., None, :] // tile_side == indices[:, None]).astype(jnp.bfloat16)
    column_match_count = (listed[..., None, :] % tile_side == indices[:, None]).astype(jnp.bfloat16)
    return jnp.einsum(
        "...am,...bm->...ab",
        row_match_count,
        column_match_count,
        preferred_element_type=jnp.float32,
    )


def warp_tiles(raw_tiles, pixel_offsets, shift_entry_index, shift_table):
    entries = shift_table.shape[0]
    tile_side = raw_tiles.shape[-1]
    selected_entries = (shift_entry_index[..., None] == jnp.arange(entries)).astype(jnp.float32)
    fraction = jnp.sum(selected_entries[..., None] * shift_table, axis=-2)
    shifts = pixel_offsets.astype(jnp.float32) + fraction
    target_positions = jnp.arange(tile_side).astype(jnp.float32)
    spacing = target_positions[:, None] - target_positions[None, :]
    row_weights = lanczos(spacing - shifts[..., 0, None, None]).astype(jnp.bfloat16)
    col_weights = lanczos(spacing - shifts[..., 1, None, None]).astype(jnp.bfloat16)
    halfway = jnp.einsum(
        "vtap,vtpq->vtaq", row_weights, raw_tiles, preferred_element_type=jnp.float32
    ).astype(jnp.bfloat16)
    return jnp.einsum(
        "vtaq,vtbq->vtab", halfway, col_weights, preferred_element_type=jnp.float32
    ).astype(jnp.bfloat16)


MESH = pl.DeviceIdType.MESH


def coadd_kernel(
    sizes, margin, sum_ref, high_ref, low_ref, tally_ref, out_ref,
    got, full, sent_parts, got_parts, sent_rows, got_rows, sent_edge, got_edge,
):
    visits, bands, patches = sizes
    n = visits * bands
    tiles, rows, lanes = sum_ref.shape
    chunk = rows // n
    me = lax.axis_index("visit") * bands + lax.axis_index("band")
    sky = lax.axis_index("sky")
    has_low, has_high = sky > 0, sky < patches - 1

    def place(k):
        peer = lax.rem(me + k, n)
        return peer, {"visit": peer // bands, "band": lax.rem(peer, bands)}

    barrier = pltpu.get_barrier_semaphore()
    for k in range(1, n):
        pl.semaphore_signal(barrier, inc=1, device_id=place(k)[1], device_id_type=MESH)

    @pl.when(has_low)
    def _():
        pl.semaphore_signal(barrier, inc=1, device_id={"sky": sky - 1}, device_id_type=MESH)

    @pl.when(has_high)
    def _():
        pl.semaphore_signal(barrier, inc=1, device_id={"sky": sky + 1}, device_id_type=MESH)

    neighbours = (sky + patches - 1) // patches + (2 * patches - 2 - sky) // patches
    pl.semaphore_wait(barrier, n - 1 + neighbours)

    parts = (sum_ref, high_ref, low_ref)
    copies = []
    for k in range(1, n):
        peer, where = place(k)
        peer_rows = pl.ds(pl.multiple_of(peer * chunk, chunk), chunk)
        for i, part in enumerate(parts):
            copy = pltpu.make_async_remote_copy(
                src_ref=part.at[:, peer_rows],
                dst_ref=got.at[k - 1, i],
                send_sem=sent_parts.at[k - 1, i],
                recv_sem=got_parts.at[k - 1, i],
                device_id=where,
                device_id_type=MESH,
            )
            copy.start()
            copies.append(copy)

    @pl.when(jnp.logical_not(has_low))
    def _():
        full[:, :margin] = jnp.zeros((tiles, margin, lanes), full.dtype)

    @pl.when(jnp.logical_not(has_high))
    def _():
        full[:, rows + margin :] = jnp.zeros((tiles, margin, lanes), full.dtype)

    own_rows = pl.ds(pl.multiple_of(me * chunk, chunk), chunk)
    total, high, low = (part[:, own_rows].astype(jnp.float32) for part in parts)
    for copy in copies:
        copy.wait_recv()
    for k in range(n - 1):
        total += got[k, 0].astype(jnp.float32)
        high = jnp.maximum(high, got[k, 1].astype(jnp.float32))
        low = jnp.minimum(low, got[k, 2].astype(jnp.float32))
    count = tally_ref[:, own_rows].astype(jnp.float32)
    full_rows = pl.ds(pl.multiple_of(margin + me * chunk, 16), chunk)
    full[:, full_rows] = ((total - high - low) / (count - 2.0)).astype(full.dtype)

    shares = []
    for k in range(1, n):
        copy = pltpu.make_async_remote_copy(
            src_ref=full.at[:, full_rows],
            dst_ref=full.at[:, full_rows],
            send_sem=sent_rows.at[k - 1],
            recv_sem=got_rows.at[k - 1],
            device_id=place(k)[1],
            device_id_type=MESH,
        )
        copy.start()
        shares.append(copy)
    for copy in copies:
        copy.wait_send()
    for copy in shares:
        copy.wait_recv()

    up = pltpu.make_async_remote_copy(
        src_ref=full.at[:, pl.ds(rows, margin)],
        dst_ref=full.at[:, pl.ds(0, margin)],
        send_sem=sent_edge.at[0],
        recv_sem=got_edge.at[0],
        device_id={"sky": lax.rem(sky + 1, patches)},
        device_id_type=MESH,
    )
    down = pltpu.make_async_remote_copy(
        src_ref=full.at[:, pl.ds(margin, margin)],
        dst_ref=full.at[:, pl.ds(rows + margin, margin)],
        send_sem=sent_edge.at[1],
        recv_sem=got_edge.at[1],
        device_id={"sky": lax.rem(sky + patches - 1, patches)},
        device_id_type=MESH,
    )

    @pl.when(has_high)
    def _():
        up.start()

    @pl.when(has_low)
    def _():
        down.start()

    side = lanes // 2
    out_ref[:, :side] = jnp.zeros((rows + 2 * margin, side), out_ref.dtype)
    out_ref[:, side + tiles * lanes :] = jnp.zeros((rows + 2 * margin, side), out_ref.dtype)

    def lay(row, count):
        image = jnp.concatenate([full[t, row : row + count] for t in range(tiles)], axis=1)
        out_ref[row : row + count, side : side + tiles * lanes] = image.astype(out_ref.dtype)

    lay(margin, rows)

    @pl.when(has_low)
    def _():
        up.wait_recv()

    @pl.when(has_high)
    def _():
        down.wait_recv()

    lay(0, margin)
    lay(rows + margin, margin)

    @pl.when(has_high)
    def _():
        up.wait_send()

    @pl.when(has_low)
    def _():
        down.wait_send()

    for copy in shares:
        copy.wait_send()


def padded_coadd(sizes, margin, partial_sums, partial_high, partial_low, tallies):
    tiles, rows, lanes = partial_sums.shape
    n = sizes[0] * sizes[1]
    return pl.pallas_call(
        functools.partial(coadd_kernel, sizes, margin),
        out_shape=jax.ShapeDtypeStruct((rows + 2 * margin, (tiles + 1) * lanes), jnp.float32),
        in_specs=[pl.BlockSpec(memory_space=pltpu.VMEM)] * 4,
        out_specs=pl.BlockSpec(memory_space=pltpu.VMEM),
        scratch_shapes=[
            pltpu.VMEM((n - 1, 3, tiles, rows // n, lanes), jnp.bfloat16),
            pltpu.VMEM((tiles, rows + 2 * margin, lanes), jnp.bfloat16),
            pltpu.SemaphoreType.DMA((n - 1, 3)),
            pltpu.SemaphoreType.DMA((n - 1, 3)),
            pltpu.SemaphoreType.DMA((n - 1,)),
            pltpu.SemaphoreType.DMA((n - 1,)),
            pltpu.SemaphoreType.DMA((2,)),
            pltpu.SemaphoreType.DMA((2,)),
        ],
        compiler_params=pltpu.CompilerParams(
            collective_id=1, has_side_effects=True, vmem_limit_bytes=24 * 2**20
        ),
    )(partial_sums, partial_high, partial_low, tallies)


def difference_kernel(basis_count, kernel_side, mix_ref, pad_ref, row_ref, slab_ref, valid_ref, out_ref, acc):
    visit_count, tiles, side, _ = slab_ref.shape
    source = lax.broadcasted_iota(jnp.int32, (side, side), 0)
    target = lax.broadcasted_iota(jnp.int32, (side, side), 1)
    first, second = source > target, source < target

    def product(dy):
        upper, lower = [], []
        for b in range(basis_count):
            row = row_ref[pl.ds(dy * basis_count + b, 1), :]
            ring = pltpu.roll(
                jnp.broadcast_to(row, (side, side)), 0, axis=1, stride=1, stride_axis=0
            )
            upper.append(jnp.where(first, ring, 0.0).astype(jnp.bfloat16))
            lower.append(jnp.where(second, ring, 0.0).astype(jnp.bfloat16))
        band = jnp.concatenate(
            [jnp.concatenate(upper, axis=1), jnp.concatenate(lower, axis=1)], axis=0
        )
        height = pad_ref.shape[0]
        turned = pltpu.roll(pad_ref[...], lax.rem(height - dy, height), axis=0)
        shifted = turned[:side].astype(jnp.bfloat16)
        windows = jnp.concatenate(
            [shifted[:, t * side : (t + 2) * side] for t in range(tiles)], axis=0
        )
        return jnp.dot(windows, band, preferred_element_type=jnp.float32)

    acc[...] = product(0)

    def step(i, carry):
        acc[...] += product(2 * i + 1) + product(2 * i + 2)
        return carry

    lax.fori_loop(0, (kernel_side - 1) // 2, step, 0)

    for t in range(tiles):
        planes = [
            acc[t * side : (t + 1) * side, b * side : (b + 1) * side]
            .astype(jnp.bfloat16)
            .astype(jnp.float32)
            for b in range(basis_count)
        ]
        for v in range(visit_count):
            template = mix_ref[v, t * basis_count] * planes[0]
            for b in range(1, basis_count):
                template += mix_ref[v, t * basis_count + b] * planes[b]
            out_ref[v, :, t * side : (t + 1) * side] = (
                (slab_ref[v, t].astype(jnp.float32) - template)
                * valid_ref[v, t].astype(jnp.float32)
            ).astype(out_ref.dtype)


def filter_and_subtract(mixture, padded, kernels, slab_tiles, valid):
    visit_count, tiles, side, _ = slab_tiles.shape
    basis_count, kernel_side = kernels.shape[:2]
    margin = kernel_side // 2
    rows = jnp.pad(kernels.astype(jnp.float32), ((0, 0), (0, 0), (0, side - kernel_side)))
    rows = jnp.roll(jnp.flip(rows, axis=2), -(side // 2 - margin - 1), axis=2)
    rows = jnp.transpose(rows, (1, 0, 2)).reshape(kernel_side * basis_count, side)
    vmem = pl.BlockSpec(memory_space=pltpu.VMEM)
    return pl.pallas_call(
        functools.partial(difference_kernel, basis_count, kernel_side),
        out_shape=jax.ShapeDtypeStruct((visit_count, side, tiles * side), jnp.bfloat16),
        in_specs=[pl.BlockSpec(memory_space=pltpu.SMEM), vmem, vmem, vmem, vmem],
        out_specs=vmem,
        scratch_shapes=[pltpu.VMEM((tiles * side, basis_count * side), jnp.float32)],
        compiler_params=pltpu.CompilerParams(vmem_limit_bytes=48 * 2**20),
    )(mixture.reshape(visit_count, tiles * basis_count), padded, rows, slab_tiles, valid)


def on_device(
    raw_tiles,
    pixel_offsets,
    shift_entry_index,
    shift_table,
    tile_routes,
    bad_pixels,
    basis_kernels,
    basis_choice,
    coef_table,
):
    visit_count, tile_cols, tile_side = (raw_tiles.shape[0], raw_tiles.shape[1], raw_tiles.shape[2])
    tile_area = tile_side * tile_side
    patches = lax.axis_size("sky")
    capacity = (visit_count * tile_cols + patches - 1) // patches + 1
    seat_count = patches * capacity
    warped = warp_tiles(raw_tiles, pixel_offsets, shift_entry_index, shift_table)
    owners = tile_routes // tile_cols
    slot_ids = tile_routes % tile_cols
    before = jnp.arange(tile_cols)[None, :] < jnp.arange(tile_cols)[:, None]
    shared = owners[:, None, :] == owners[:, :, None]
    queue_rank = jnp.sum(shared & before[None], axis=2)
    seat_ids = owners * capacity + queue_rank
    layout = seat_ids[:, None, :] == jnp.arange(seat_count)[None, :, None]
    outgoing = jnp.einsum(
        "vsk,vkx->vsx",
        layout.astype(jnp.bfloat16),
        warped.reshape(visit_count, tile_cols, tile_area),
        preferred_element_type=jnp.float32,
    ).astype(jnp.bfloat16)
    labels = (jnp.sum(jnp.where(layout, slot_ids[:, None, :] + 1, 0), axis=2) - 1).astype(
        jnp.bfloat16
    )
    arrived, arrived_labels = (
        lax.all_to_all(
            outgoing.reshape(visit_count, patches, capacity * tile_area),
            "sky",
            split_axis=1,
            concat_axis=1,
            tiled=True,
        ),
        lax.all_to_all(
            labels.reshape(visit_count, patches, capacity),
            "sky",
            split_axis=1,
            concat_axis=1,
            tiled=True,
        ),
    )
    landing = (
        arrived_labels.astype(jnp.float32).reshape(visit_count, seat_count)[:, None, :]
        == jnp.arange(tile_cols).astype(jnp.float32)[None, :, None]
    )
    placed = jnp.einsum(
        "vks,vsx->vkx",
        landing.astype(jnp.bfloat16),
        arrived.reshape(visit_count, seat_count, tile_area),
        preferred_element_type=jnp.float32,
    ).astype(jnp.bfloat16)
    slab_tiles = placed.reshape(visit_count, tile_cols, tile_side, tile_side)
    sizes = tuple(lax.axis_size(axis) for axis in ("visit", "band", "sky"))
    shard_index = lax.axis_index(("visit", "band"))
    visit_total = bad_pixels.shape[0]
    listed_count = bad_pixels.shape[2]
    own_listed = lax.dynamic_slice_in_dim(bad_pixels, shard_index * visit_count, visit_count, 0)
    valid_pixel_mask = 1.0 - hit_planes(own_listed, tile_side)
    all_listed = jnp.transpose(bad_pixels, (1, 0, 2)).reshape(
        tile_cols, visit_total * listed_count
    )
    tallies = (visit_total - hit_planes(all_listed, tile_side)).astype(jnp.bfloat16)
    values = slab_tiles.astype(jnp.float32)
    partial_sums = jnp.sum(valid_pixel_mask * values, axis=0).astype(jnp.bfloat16)
    partial_high = jnp.max(jnp.where(valid_pixel_mask > 0.5, slab_tiles, -jnp.inf), axis=0)
    partial_low = jnp.min(jnp.where(valid_pixel_mask > 0.5, slab_tiles, jnp.inf), axis=0)
    margin = basis_kernels.shape[-1] // 2
    padded = padded_coadd(sizes, margin, partial_sums, partial_high, partial_low, tallies)
    entries = coef_table.shape[0]
    picks = (basis_choice[..., None] == jnp.arange(entries)).astype(jnp.float32)
    mixture = jnp.sum(picks[..., None] * coef_table, axis=2)
    return filter_and_subtract(
        mixture, padded, basis_kernels, slab_tiles, valid_pixel_mask.astype(jnp.bfloat16)
    )


def solution(mesh):
    return jax.shard_map(
        on_device,
        mesh=mesh,
        in_specs=(
            P(("group", "visit", "band"), "sky", None, None),
            P(("group", "visit", "band"), "sky", None),
            P(("group", "visit", "band"), "sky"),
            P(),
            P(("group", "visit", "band"), "sky"),
            P("group", "sky", None),
            P(),
            P(("group", "visit", "band"), "sky"),
            P(),
        ),
        out_specs=P(("group", "visit", "band"), "sky", None),
        check_vma=False,
    )
```

time: 323 us -> 99.2 us (0.31)
  local copies, waits for them, and re-layouts: 196 us -> 9.47 us
  Pallas kernels: 0 us -> 36.4 us
  waiting for transfers between devices: 54.8 us -> 29.5 us
  matrix products: 31.6 us -> 7.71 us
  between operations: 13.5 us -> 0.2 us
  other arithmetic: 10 us -> 4.03 us
  starting transfers between devices: 14.9 us -> 11.6 us
    gather x2 -> x0, local copies, waits for them, and re-layouts: 147 us -> none  [banded_filter(): bands = jnp.take(kernels, jnp.clip(offsets, 0, kernel_side - 1), axis=2)]
    pallas_call x0 -> x2, Pallas kernels: none -> 36.4 us  [the longest x1 20 us: filter_and_subtract(): pl.pallas_call(functools.partial(difference_kernel, basis_count, kernel_s...]
    while x257 -> x0, local copies, waits for them, and re-layouts: 29.8 us -> none
    dot_general x9 -> x0, matrix products: 22.2 us -> none  [the longest x8 19.5 us: one_tile(): jnp.einsum('adx,bdxc->bac', shifted, bands, preferred_element_type=jnp.fl...]
    all_gather x1 -> x0, waiting for transfers between devices: 20.7 us -> none  [on_device(): lax.all_gather(banded_filter(padded, own_kernels, tile_side, tile_cols),...]
    ppermute x2 -> x0, starting transfers between devices: 3.28 us -> none  [the longest x1 2 us: with_halo(): lax.ppermute(lax.slice_in_dim(block, block.shape[dim] - width, None, axis...]
  transfers between devices with their start and end apart: 8 -> 2, of which waited for: 3 -> 1; matrix products, arithmetic and copies ran while one was open for 52% -> 14% of each run, Pallas kernels for 0% -> 0%
where the time goes in v2:
time: 99.2 us; the launch traced here: 98.8 us
  Pallas kernels  36.4 us (37%)
  waiting for transfers between devices  29.5 us (30%)
  starting transfers between devices  11.6 us (12%)
  local copies, waits for them, and re-layouts  9.47 us (10%)
  matrix products  7.71 us (8%)
  other arithmetic  4.03 us (4%)
    all_to_all x1, waiting for transfers between devices, on_device(): lax.all_to_all(outgoing.reshape(visit_count, patches, capacity * tile_are...  29.5 us
    pallas_call x1, Pallas kernels, filter_and_subtract(): pl.pallas_call(functools.partial(difference_kernel, basis_count, kernel_s...  20 us
    pallas_call x1, Pallas kernels, padded_coadd(): pl.pallas_call(functools.partial(coadd_kernel, sizes, margin), out_shape=...  16.4 us
    all_to_all x1, starting transfers between devices, on_device(): lax.all_to_all(labels.reshape(visit_count, patches, capacity), 'sky', spl...  6.32 us
    all_to_all x1, starting transfers between devices, on_device(): lax.all_to_all(outgoing.reshape(visit_count, patches, capacity * tile_are...  5.24 us
    dot_general x1, matrix products, warp_tiles(): jnp.einsum('vtaq,vtbq->vtab', halfway, col_weights, preferred_element_typ...  5.17 us
    reshape x2, local copies, waits for them, and re-layouts, on_device(): outgoing.reshape(visit_count, patches, capacity * tile_area)  3.98 us
    all_to_all x1, local copies, waits for them, and re-layouts, on_device(): lax.all_to_all(outgoing.reshape(visit_count, patches, capacity * tile_are...  2.08 us
  transfers between devices with their start and end apart: 2, of which 1 were waited for; matrix products, arithmetic and copies ran while one was open for 14% of the time, Pallas kernels for 0%

profile of v2, /device:TPU:0, one launch (start us, length us, event | category | flops | bytes accessed | tf_op | source)
XLA Modules:
  0.0 98.8 jit_solution(18119413743701948671)
XLA Ops:
  0.0 0.7 fusion.146
  0.8 0.2 convert_reduce_fusion
  1.0 0.1 select_reduce_fusion
  1.1 0.1 convert_element_type.96
  1.2 0.6 copy.29
  1.8 6.3 %all-to-all-start = ((bf16[2,4,5]{2,0,1:T(2,128)(2,1)}), bf16[2,4,5]{2,0,1:T(2,128)(2,1)S(1)}, u32[]{:S(2)}, u32[]{:S(2)}) async-start(bf16[2,4,5]{2,0,1:T(2,128)(2,1)} %copy.29), calls=%async_computation | async-start | bytes 4096 | tf_op jit(solution)/shard_map/all_to_all | solution.py:325
  8.1 0.7 fusion.139
  8.8 0.8 multiply_reduce_fusion.2
  9.6 0.7 convert_add_fusion
  10.3 0.1 broadcast_subtract_fusion
  10.4 5.2 %convolution_convert_fusion.2 = bf16[2,8,128,128]{3,2,1,0:T(8,128)(2,1)S(1)} fusion(bf16[2,8,128,128]{3,2,1,0:T(8,128)(2,1)S(1)} %copy-done, f32[2,8]{1,0:T(2,128)S(1)} %bitcast.24, f32[2,8]{1,0:T(2,128)S(1)} %bitcast.23, f32[128,128]{1,0:T(8,128)S(1)} %broadcast_subtract_fusion), kind=kOutput, calls=%fused_computation.49 | convolution fusion | flops 172490752 | bytes 1114240 | tf_op jit(solution)/shard_map/vtaq,vtbq->vtab/dot_general | solution.py:40
  15.6 0.2 reshape.208
  15.8 0.7 convolution_convert_fusion
  16.5 1.6 %reshape.209 = bf16[2,4,81920]{2,1,0:T(4,128)(2,1)S(1)} reshape(bf16[2,20,16384]{2,1,0:T(8,128)(2,1)S(1)} %convolution_convert_fusion) | data formatting | bytes 2621440 | tf_op jit(solution)/shard_map/reshape | solution.py:319
  18.0 2.4 %copy.31 = bf16[2,4,81920]{2,0,1:T(2,128)(2,1)} copy(bf16[2,4,81920]{2,1,0:T(4,128)(2,1)S(1)} %reshape.209) | data formatting | bytes 2621440 | tf_op jit(solution)/shard_map/reshape | solution.py:319
  20.5 5.2 %all-to-all-start.1 = ((bf16[2,4,81920]{2,0,1:T(2,128)(2,1)}), bf16[2,4,81920]{2,0,1:T(2,128)(2,1)S(1)}, u32[]{:S(2)}, u32[]{:S(2)}) async-start(bf16[2,4,81920]{2,0,1:T(2,128)(2,1)} %copy.31), calls=%async_computation.1 | async-start | bytes 2621440 | tf_op jit(solution)/shard_map/all_to_all | solution.py:318
  25.8 0.1 multiply_reduce_fusion.1
  25.9 0.1 copy.28
  26.0 0.1 reshape.207.mix_ref
  26.1 0.1 broadcast_in_dim_reshape.2
  26.2 0.1 slice.23
  26.5 0.4 fusion.27.tally_ref
  26.9 0.1 reshape.213
  27.0 29.5 %all-to-all-done.1 = bf16[2,4,81920]{2,0,1:T(2,128)(2,1)S(1)} async-done(((bf16[2,4,81920]{2,0,1:T(2,128)(2,1)}), bf16[2,4,81920]{2,0,1:T(2,128)(2,1)S(1)}, u32[]{:S(2)}, u32[]{:S(2)}) %all-to-all-start.1) | async-done | bytes 1310752 | tf_op jit(solution)/shard_map/all_to_all | solution.py:318
  56.5 2.1 %copy.32 = bf16[2,4,81920]{2,1,0:T(4,128)(2,1)} copy(bf16[2,4,81920]{2,0,1:T(2,128)(2,1)S(1)} %all-to-all-done.1) | data formatting | bytes 2621440 | tf_op jit(solution)/shard_map/all_to_all | solution.py:318
  58.6 2.0 %reshape.210 = bf16[2,20,16384]{2,1,0:T(8,128)(2,1)S(1)} reshape(bf16[2,4,81920]{2,1,0:T(4,128)(2,1)} %copy.32) | data formatting | bytes 2621440 | tf_op jit(solution)/shard_map/reshape | solution.py:340
  60.6 0.5 fusion.26
  61.0 1.0 fusion.173
  62.0 0.1 fusion.134
  62.2 0.3 fusion.100
  62.5 16.4 %shard_map.91.pad_ref = f32[160,1152]{1,0:T(8,128)S(1)} custom-call(bf16[8,128,128]{2,1,0:T(8,128)(2,1)S(1)} %get-tuple-element.11.sum_ref, bf16[8,128,128]{2,1,0:T(8,128)(2,1)S(1)} %get-tuple-element.7.high_ref, bf16[8,128,128]{2,1,0:T(8,128)(2,1)S(1)} %get-tuple-element.6.low_ref, bf16[8,128,128]{2,1,0:T(8,128)(2,1)S(1)} %fusion.27.tally_ref), custom_call_target="tpu_custom_call" | custom-call | tf_op jit(solution)/shard_map/pallas_call | solution.py:194
  78.9 20.0 %shard_map.92 = bf16[2,128,1024]{2,1,0:T(8,128)(2,1)} custom-call(f32[2,32]{1,0:T(2,128)S(1)} %reshape.207.mix_ref, f32[160,1152]{1,0:T(8,128)S(1)} %shard_map.91.pad_ref, f32[132,128]{1,0:T(8,128)S(1)} %reshape.212.row_ref, bf16[2,8,128,128]{3,2,1,0:T(8,128)(2,1)S(1)} %get-tuple-element.12.slab_ref, bf16[2,8,128,128]{3,2,1,0:T(8,128)(2,1)S(1)} %get-tuple-element.10.valid_ref), custom_call_target="tpu_custom_call" | custom-call | tf_op jit(solution)/shard_map/pallas_call | solution.py:274
  (26 shorter events, 0.3 us)
Async XLA Ops:
  0.0 10.4 %copy-start = (bf16[2,8,128,128]{3,2,1,0:T(8,128)(2,1)S(1)}, bf16[2,8,128,128]{3,2,1,0:T(8,128)(2,1)}, u32[]{:S(2)}) copy-start(bf16[2,8,128,128]{3,2,1,0:T(8,128)(2,1)} %param.10) | copy-start | bytes 1572868
  1.8 18.7 %all-to-all-start = ((bf16[2,4,5]{2,0,1:T(2,128)(2,1)}), bf16[2,4,5]{2,0,1:T(2,128)(2,1)S(1)}, u32[]{:S(2)}, u32[]{:S(2)}) async-start(bf16[2,4,5]{2,0,1:T(2,128)(2,1)} %copy.29), calls=%async_computation | async-start | bytes 4096 | tf_op jit(solution)/shard_map/all_to_all | solution.py:325
  20.5 5.3 %copy-start.4 = (s32[2,8]{1,0:T(2,128)S(1)}, s32[2,8]{1,0:T(2,128)}, u32[]{:S(2)}) copy-start(s32[2,8]{1,0:T(2,128)} %param.17) | copy-start | bytes 196
  20.5 5.3 %copy-start.3 = (f32[16,4]{0,1:T(4,128)S(1)}, f32[16,4]{0,1:T(4,128)}, u32[]{:S(2)}) copy-start(f32[16,4]{0,1:T(4,128)} %param.18) | copy-start | bytes 772
  20.5 5.6 %copy-start.1 = (s32[8,8,32]{2,1,0:T(8,128)S(1)}, s32[8,8,32]{2,1,0:T(8,128)}, u32[]{:S(2)}) copy-start(s32[8,8,32]{2,1,0:T(8,128)} %param.15) | copy-start | bytes 24580
  20.5 5.7 %copy-start.2 = (bf16[4,33,33]{2,0,1:T(4,128)(2,1)S(1)}, bf16[4,33,33]{2,0,1:T(4,128)(2,1)}, u32[]{:S(2)}) copy-start(bf16[4,33,33]{2,0,1:T(4,128)(2,1)} %param.16) | copy-start | bytes 26140
  20.5 36.0 %all-to-all-start.1 = ((bf16[2,4,81920]{2,0,1:T(2,128)(2,1)}), bf16[2,4,81920]{2,0,1:T(2,128)(2,1)S(1)}, u32[]{:S(2)}, u32[]{:S(2)}) async-start(bf16[2,4,81920]{2,0,1:T(2,128)(2,1)} %copy.31), calls=%async_computation.1 | async-start | bytes 2621440 | tf_op jit(solution)/shard_map/all_to_all | solution.py:318

commit v3 on v2

--- a/solution.py
+++ b/solution.py
@@ -212,6 +212,121 @@
     )(partial_sums, partial_high, partial_low, tallies)
 
 
+def exchange_kernel(
+    source_ref, warped_ref, label_ref, out_ref, out_label_ref,
+    stage, landed, landed_labels, sent, received, sent_labels, received_labels,
+):
+    patches, capacity = stage.shape[:2]
+    sky = lax.axis_index("sky")
+    barrier = pltpu.get_barrier_semaphore()
+    for k in range(1, patches):
+        peer = lax.rem(sky + k, patches)
+        pl.semaphore_signal(barrier, inc=1, device_id={"sky": peer}, device_id_type=MESH)
+    for k in range(patches):
+        block = lax.rem(sky + k, patches)
+        for c in range(capacity):
+            stage[k, c] = warped_ref[source_ref[block * capacity + c]]
+    pl.semaphore_wait(barrier, patches - 1)
+    copies = []
+    for k in range(1, patches):
+        peer = lax.rem(sky + k, patches)
+        for src, dst, gone, come in (
+            (stage.at[k], landed.at[k], sent, received),
+            (label_ref.at[peer], landed_labels.at[k], sent_labels, received_labels),
+        ):
+            copy = pltpu.make_async_remote_copy(
+                src_ref=src,
+                dst_ref=dst,
+                send_sem=gone.at[k],
+                recv_sem=come.at[k],
+                device_id={"sky": peer},
+                device_id_type=MESH,
+            )
+            copy.start()
+            copies.append(copy)
+    out_ref[0] = stage[0]
+    out_label_ref[0] = label_ref[sky]
+    for i, copy in enumerate(copies):
+        copy.wait_recv()
+        k = i // 2 + 1
+        if i % 2 == 0:
+            out_ref[k] = landed[k]
+        else:
+            out_label_ref[k] = landed_labels[k]
+    for copy in copies:
+        copy.wait_send()
+
+
+def exchange_tiles(sources, warped, labels):
+    patches, capacity = labels.shape
+    side = warped.shape[-1]
+    spread = jnp.pad(
+        labels.astype(jnp.bfloat16)[:, None, :], ((0, 0), (0, 15), (0, side - capacity))
+    )
+    vmem = pl.BlockSpec(memory_space=pltpu.VMEM)
+    tiles = (patches, capacity, side, side)
+    arrived, arrived_labels = pl.pallas_call(
+        exchange_kernel,
+        out_shape=(
+            jax.ShapeDtypeStruct(tiles, jnp.bfloat16),
+            jax.ShapeDtypeStruct(spread.shape, jnp.bfloat16),
+        ),
+        in_specs=[pl.BlockSpec(memory_space=pltpu.SMEM), vmem, vmem],
+        out_specs=(vmem, vmem),
+        scratch_shapes=[
+            pltpu.VMEM(tiles, jnp.bfloat16),
+            pltpu.VMEM(tiles, jnp.bfloat16),
+            pltpu.VMEM(spread.shape, jnp.bfloat16),
+            pltpu.SemaphoreType.DMA((patches,)),
+            pltpu.SemaphoreType.DMA((patches,)),
+            pltpu.SemaphoreType.DMA((patches,)),
+            pltpu.SemaphoreType.DMA((patches,)),
+        ],
+        compiler_params=pltpu.CompilerParams(
+            collective_id=2, has_side_effects=True, vmem_limit_bytes=32 * 2**20
+        ),
+    )(sources, warped, spread)
+    return arrived, arrived_labels[:, 0, :capacity]
+
+
+def place_kernel(seat_ref, arrived_ref, valid_ref, slab_ref, sum_ref, high_ref, low_ref):
+    visit_count, tiles = slab_ref.shape[:2]
+
+    def step(t, carry):
+        total = high = low = None
+        for v in range(visit_count):
+            tile = arrived_ref[seat_ref[v * tiles + t]]
+            slab_ref[v, t] = tile
+            value = tile.astype(jnp.float32)
+            usable = valid_ref[v, t].astype(jnp.float32)
+            at_most = jnp.where(usable > 0.5, value, -jnp.inf)
+            at_least = jnp.where(usable > 0.5, value, jnp.inf)
+            if total is None:
+                total, high, low = usable * value, at_most, at_least
+            else:
+                total = total + usable * value
+                high, low = jnp.maximum(high, at_most), jnp.minimum(low, at_least)
+        sum_ref[t] = total.astype(sum_ref.dtype)
+        high_ref[t] = high.astype(high_ref.dtype)
+        low_ref[t] = low.astype(low_ref.dtype)
+        return carry
+
+    lax.fori_loop(0, tiles, step, 0)
+
+
+def place_tiles(seats, arrived, valid):
+    visit_count, tiles, side, _ = valid.shape
+    vmem = pl.BlockSpec(memory_space=pltpu.VMEM)
+    plane = jax.ShapeDtypeStruct((tiles, side, side), jnp.bfloat16)
+    return pl.pallas_call(
+        place_kernel,
+        out_shape=(jax.ShapeDtypeStruct(valid.shape, jnp.bfloat16), plane, plane, plane),
+        in_specs=[pl.BlockSpec(memory_space=pltpu.SMEM), vmem, vmem],
+        out_specs=(vmem,) * 4,
+        compiler_params=pltpu.CompilerParams(vmem_limit_bytes=24 * 2**20),
+    )(seats, arrived, valid)
+
+
 def difference_kernel(basis_count, kernel_side, mix_ref, pad_ref, row_ref, slab_ref, valid_ref, out_ref, acc):
     visit_count, tiles, side, _ = slab_ref.shape
     source = lax.broadcasted_iota(jnp.int32, (side, side), 0)
@@ -293,54 +408,25 @@
     coef_table,
 ):
     visit_count, tile_cols, tile_side = (raw_tiles.shape[0], raw_tiles.shape[1], raw_tiles.shape[2])
-    tile_area = tile_side * tile_side
     patches = lax.axis_size("sky")
-    capacity = (visit_count * tile_cols + patches - 1) // patches + 1
-    seat_count = patches * capacity
+    pooled = visit_count * tile_cols
+    capacity = (pooled + patches - 1) // patches + 1
+    owners = (tile_routes // tile_cols).reshape(pooled)
+    slots = (tile_routes % tile_cols + tile_cols * jnp.arange(visit_count)[:, None]).reshape(pooled)
+    order = jnp.arange(pooled)
+    earlier = (owners[None, :] == owners[:, None]) & (order[None, :] < order[:, None])
+    seat_ids = owners * capacity + jnp.sum(earlier, axis=1)
+    layout = seat_ids[None, :] == jnp.arange(patches * capacity)[:, None]
+    sources = jnp.sum(jnp.where(layout, order[None, :], 0), axis=1)
+    labels = jnp.sum(jnp.where(layout, slots[None, :] + 1, 0), axis=1) - 1
     warped = warp_tiles(raw_tiles, pixel_offsets, shift_entry_index, shift_table)
-    owners = tile_routes // tile_cols
-    slot_ids = tile_routes % tile_cols
-    before = jnp.arange(tile_cols)[None, :] < jnp.arange(tile_cols)[:, None]
-    shared = owners[:, None, :] == owners[:, :, None]
-    queue_rank = jnp.sum(shared & before[None], axis=2)
-    seat_ids = owners * capacity + queue_rank
-    layout = seat_ids[:, None, :] == jnp.arange(seat_count)[None, :, None]
-    outgoing = jnp.einsum(
-        "vsk,vkx->vsx",
-        layout.astype(jnp.bfloat16),
-        warped.reshape(visit_count, tile_cols, tile_area),
-        preferred_element_type=jnp.float32,
-    ).astype(jnp.bfloat16)
-    labels = (jnp.sum(jnp.where(layout, slot_ids[:, None, :] + 1, 0), axis=2) - 1).astype(
-        jnp.bfloat16
-    )
-    arrived, arrived_labels = (
-        lax.all_to_all(
-            outgoing.reshape(visit_count, patches, capacity * tile_area),
-            "sky",
-            split_axis=1,
-            concat_axis=1,
-            tiled=True,
-        ),
-        lax.all_to_all(
-            labels.reshape(visit_count, patches, capacity),
-            "sky",
-            split_axis=1,
-            concat_axis=1,
-            tiled=True,
-        ),
-    )
-    landing = (
-        arrived_labels.astype(jnp.float32).reshape(visit_count, seat_count)[:, None, :]
-        == jnp.arange(tile_cols).astype(jnp.float32)[None, :, None]
-    )
-    placed = jnp.einsum(
-        "vks,vsx->vkx",
-        landing.astype(jnp.bfloat16),
-        arrived.reshape(visit_count, seat_count, tile_area),
-        preferred_element_type=jnp.float32,
-    ).astype(jnp.bfloat16)
-    slab_tiles = placed.reshape(visit_count, tile_cols, tile_side, tile_side)
+    arrived, arrived_labels = exchange_tiles(
+        sources,
+        warped.reshape(pooled, tile_side, tile_side),
+        labels.reshape(patches, capacity),
+    )
+    landing = arrived_labels.astype(jnp.float32).reshape(1, -1) == order.astype(jnp.float32)[:, None]
+    seats = jnp.sum(jnp.where(landing, jnp.arange(patches * capacity)[None, :], 0), axis=1)
     sizes = tuple(lax.axis_size(axis) for axis in ("visit", "band", "sky"))
     shard_index = lax.axis_index(("visit", "band"))
     visit_total = bad_pixels.shape[0]
@@ -351,17 +437,17 @@
         tile_cols, visit_total * listed_count
     )
     tallies = (visit_total - hit_planes(all_listed, tile_side)).astype(jnp.bfloat16)
-    values = slab_tiles.astype(jnp.float32)
-    partial_sums = jnp.sum(valid_pixel_mask * values, axis=0).astype(jnp.bfloat16)
-    partial_high = jnp.max(jnp.where(valid_pixel_mask > 0.5, slab_tiles, -jnp.inf), axis=0)
-    partial_low = jnp.min(jnp.where(valid_pixel_mask > 0.5, slab_tiles, jnp.inf), axis=0)
+    valid = valid_pixel_mask.astype(jnp.bfloat16)
+    slab_tiles, partial_sums, partial_high, partial_low = place_tiles(
+        seats, arrived.reshape(patches * capacity, tile_side, tile_side), valid
+    )
     margin = basis_kernels.shape[-1] // 2
     padded = padded_coadd(sizes, margin, partial_sums, partial_high, partial_low, tallies)
     entries = coef_table.shape[0]
     picks = (basis_choice[..., None] == jnp.arange(entries)).astype(jnp.float32)
     mixture = jnp.sum(picks[..., None] * coef_table, axis=2)
     return filter_and_subtract(
-        mixture, padded, basis_kernels, slab_tiles, valid_pixel_mask.astype(jnp.bfloat16)
+        mixture, padded, basis_kernels, slab_tiles, valid
     )
 
 

time: 99.2 us -> 72.9 us (0.73)
  waiting for transfers between devices: 29.5 us -> 0 us
  Pallas kernels: 36.4 us -> 59.8 us
  starting transfers between devices: 11.6 us -> 0 us
  local copies, waits for them, and re-layouts: 9.47 us -> 4.64 us
  other arithmetic: 4.03 us -> 1.8 us
  matrix products: 7.71 us -> 6.23 us
    all_to_all x2 -> x0, waiting for transfers between devices: 29.5 us -> none  [the longest x1 29.5 us: on_device(): lax.all_to_all(outgoing.reshape(visit_count, patches, capacity * tile_are...]
    pallas_call x0 -> x2, Pallas kernels: none -> 18.6 us  [the longest x1 17.6 us: exchange_tiles(): pl.pallas_call(exchange_kernel, out_shape=(jax.ShapeDtypeStruct(tiles, jn...]
    all_to_all x2 -> x0, starting transfers between devices: 11.6 us -> none  [the longest x1 6.32 us: on_device(): lax.all_to_all(labels.reshape(visit_count, patches, capacity), 'sky', spl...]
    reshape x4 -> x1, local copies, waits for them, and re-layouts: 6.17 us -> 0.08 us  [on_device(): owners = (tile_routes // tile_cols).reshape(pooled)]
    pallas_call x1, Pallas kernels: 16.4 us -> 21 us  [padded_coadd(): pl.pallas_call(functools.partial(coadd_kernel, sizes, margin), out_shape=...]
    unnamed x10 -> x18, local copies, waits for them, and re-layouts: 0.02 us -> 3.85 us
    all_to_all x1 -> x0, local copies, waits for them, and re-layouts: 2.08 us -> none  [on_device(): lax.all_to_all(outgoing.reshape(visit_count, patches, capacity * tile_are...]
    dot_general x2 -> x0, matrix products: 1.14 us -> none  [the longest x1 0.67 us: on_device(): jnp.einsum('vsk,vkx->vsx', layout.astype(jnp.bfloat16), warped.reshape(vi...]
  transfers between devices with their start and end apart: 2 -> 0, of which waited for: 1 -> 0; matrix products, arithmetic and copies ran while one was open for 14% -> 0% of each run, Pallas kernels for 0% -> 0%
where the time goes in v3:
time: 72.9 us; the launch traced here: 72.6 us
  Pallas kernels  59.8 us (82%)
  matrix products  6.23 us (9%)
  local copies, waits for them, and re-layouts  4.64 us (6%)
  other arithmetic  1.8 us (2%)
    pallas_call x1, Pallas kernels, padded_coadd(): pl.pallas_call(functools.partial(coadd_kernel, sizes, margin), out_shape=...  21 us
    pallas_call x1, Pallas kernels, filter_and_subtract(): pl.pallas_call(functools.partial(difference_kernel, basis_count, kernel_s...  20.2 us
    pallas_call x1, Pallas kernels, exchange_tiles(): pl.pallas_call(exchange_kernel, out_shape=(jax.ShapeDtypeStruct(tiles, jn...  17.6 us
    dot_general x1, matrix products, warp_tiles(): jnp.einsum('vtaq,vtbq->vtab', halfway, col_weights, preferred_element_typ...  5.17 us
    unnamed x18, local copies, waits for them, and re-layouts  3.85 us

profile of v3, /device:TPU:0, one launch (start us, length us, event | category | flops | bytes accessed | tf_op | source)
XLA Modules:
  0.0 72.6 jit_solution(10868819026370061982)
XLA Ops:
  0.0 0.8 %add_select_fusion.3 = (s32[2,8,32]{2,1,0:T(8,128)S(1)}, pred[2,8,32]{2,1,0:T(8,128)(4,1)S(1)}) fusion(s32[8,8,32]{2,1,0:T(8,128)} %param.15, s32[]{:T(128)S(6)} %select_n.91), kind=kLoop, calls=%fused_computation.161 | loop fusion | flops 7680 | bytes 4612 | tf_op jit(solution)/shard_map/jit(floor_divide)/jit(_where)/select_n | solution.py:17
  0.8 0.0 copy-done.1
  0.8 0.6 fusion.26.valid_ref
  1.5 0.7 copy-done.5
  2.2 0.1 and_select_fusion.1
  2.2 0.1 reshape.232
  2.3 0.2 convert_reduce_fusion
  2.5 0.1 add.129
  2.6 0.1 select_reduce_fusion.1
  2.7 0.1 convert_element_type.110
  2.8 0.7 copy-done.6
  3.5 0.1 fusion.134
  3.5 0.6 copy-done.8
  4.2 0.1 multiply_reduce_fusion.1
  4.2 0.6 copy-done.3
  4.9 0.1 broadcast_subtract_fusion
  5.0 5.2 %convolution_convert_fusion = bf16[2,8,128,128]{3,2,1,0:T(8,128)(2,1)S(1)} fusion(bf16[2,8,128,128]{3,2,1,0:T(8,128)(2,1)S(1)} %copy-done, f32[2,8]{1,0:T(2,128)S(1)} %bitcast.12, f32[2,8]{1,0:T(2,128)S(1)} %bitcast.11, f32[128,128]{1,0:T(8,128)S(1)} %broadcast_subtract_fusion), kind=kOutput, calls=%fused_computation.48 | convolution fusion | flops 172490752 | bytes 1114240 | tf_op jit(solution)/shard_map/vtaq,vtbq->vtab/dot_general | solution.py:40
  10.1 17.6 %shard_map.91 = (bf16[4,5,128,128]{3,2,1,0:T(8,128)(2,1)S(1)}, bf16[4,16,128]{2,1,0:T(8,128)(2,1)S(1)}) custom-call(s32[20]{0:T(128)S(1)} %get-tuple-element.19.source_ref, bf16[16,128,128]{2,1,0:T(8,128)(2,1)S(1)} %bitcast.9, bf16[4,16,128]{2,1,0:T(8,128)(2,1)S(1)} %pad.10.label_ref), custom_call_target="tpu_custom_call" | custom-call | tf_op jit(solution)/shard_map/pallas_call | solution.py:268
  27.7 0.1 reshape.236
  27.8 0.2 select_reduce_fusion.seat_ref
  28.0 1.0 %shard_map.92 = (bf16[2,8,128,128]{3,2,1,0:T(8,128)(2,1)S(1)}, bf16[8,128,128]{2,1,0:T(8,128)(2,1)S(1)}, bf16[8,128,128]{2,1,0:T(8,128)(2,1)S(1)}, bf16[8,128,128]{2,1,0:T(8,128)(2,1)S(1)}) custom-call(s32[16]{0:T(128)S(1)} %select_reduce_fusion.seat_ref, bf16[20,128,128]{2,1,0:T(8,128)(2,1)S(1)} %bitcast.8, bf16[2,8,128,128]{3,2,1,0:T(8,128)(2,1)S(1)} %fusion.26.valid_ref), custom_call_target="tpu_custom_call" | custom-call | tf_op jit(solution)/shard_map/pallas_call | solution.py:321
  29.0 0.1 broadcast_in_dim_reshape.2
  29.1 0.4 fusion.27.tally_ref
  29.6 21.0 %shard_map.93.pad_ref = f32[160,1152]{1,0:T(8,128)S(1)} custom-call(bf16[8,128,128]{2,1,0:T(8,128)(2,1)S(1)} %get-tuple-element.14.sum_ref, bf16[8,128,128]{2,1,0:T(8,128)(2,1)S(1)} %get-tuple-element.15.high_ref, bf16[8,128,128]{2,1,0:T(8,128)(2,1)S(1)} %get-tuple-element.16.low_ref, bf16[8,128,128]{2,1,0:T(8,128)(2,1)S(1)} %fusion.27.tally_ref), custom_call_target="tpu_custom_call" | custom-call | tf_op jit(solution)/shard_map/pallas_call | solution.py:194
  50.6 0.1 slice.27
  50.8 0.6 copy-done.7
  51.4 0.1 fusion.132
  51.5 0.6 copy-done.4
  52.1 0.1 multiply_reduce_fusion
  52.2 0.1 copy.17
  52.3 0.1 reshape.231.mix_ref
  52.4 20.2 %shard_map.94 = bf16[2,128,1024]{2,1,0:T(8,128)(2,1)} custom-call(f32[2,32]{1,0:T(2,128)S(1)} %reshape.231.mix_ref, f32[160,1152]{1,0:T(8,128)S(1)} %shard_map.93.pad_ref, f32[132,128]{1,0:T(8,128)S(1)} %reshape.235.row_ref, bf16[2,8,128,128]{3,2,1,0:T(8,128)(2,1)S(1)} %get-tuple-element.17.slab_ref, bf16[2,8,128,128]{3,2,1,0:T(8,128)(2,1)S(1)} %fusion.26.valid_ref), custom_call_target="tpu_custom_call" | custom-call | tf_op jit(solution)/shard_map/pallas_call | solution.py:389
  (26 shorter events, 0.2 us)
Async XLA Ops:
  0.0 4.9 %copy-start = (bf16[2,8,128,128]{3,2,1,0:T(8,128)(2,1)S(1)}, bf16[2,8,128,128]{3,2,1,0:T(8,128)(2,1)}, u32[]{:S(2)}) copy-start(bf16[2,8,128,128]{3,2,1,0:T(8,128)(2,1)} %param.10) | copy-start | bytes 1572868
  0.0 0.8 %copy-start.1 = (s32[8,8,32]{2,1,0:T(8,128)S(1)}, s32[8,8,32]{2,1,0:T(8,128)}, u32[]{:S(2)}) copy-start(s32[8,8,32]{2,1,0:T(8,128)} %param.15) | copy-start | bytes 24580
  1.5 0.7 copy-start.5
  2.8 0.7 copy-start.6
  3.5 0.7 copy-start.8
  4.2 0.7 copy-start.3
  29.5 21.0 %copy-start.2 = (bf16[4,33,33]{2,0,1:T(4,128)(2,1)S(1)}, bf16[4,33,33]{2,0,1:T(4,128)(2,1)}, u32[]{:S(2)}) copy-start(bf16[4,33,33]{2,0,1:T(4,128)(2,1)} %param.16) | copy-start | bytes 26140
  50.7 0.7 copy-start.7
  51.4 0.7 copy-start.4

commit v4 on v3

--- a/solution.py
+++ b/solution.py
@@ -327,13 +327,13 @@
     )(seats, arrived, valid)
 
 
-def difference_kernel(basis_count, kernel_side, mix_ref, pad_ref, row_ref, slab_ref, valid_ref, out_ref, acc):
+def difference_kernel(basis_count, kernel_side, mix_ref, pad_ref, row_ref, slab_ref, valid_ref, out_ref, acc, turned):
     visit_count, tiles, side, _ = slab_ref.shape
     source = lax.broadcasted_iota(jnp.int32, (side, side), 0)
     target = lax.broadcasted_iota(jnp.int32, (side, side), 1)
     first, second = source > target, source < target
 
-    def product(dy):
+    def band_of(dy):
         upper, lower = [], []
         for b in range(basis_count):
             row = row_ref[pl.ds(dy * basis_count + b, 1), :]
@@ -342,24 +342,31 @@
             )
             upper.append(jnp.where(first, ring, 0.0).astype(jnp.bfloat16))
             lower.append(jnp.where(second, ring, 0.0).astype(jnp.bfloat16))
-        band = jnp.concatenate(
-            [jnp.concatenate(upper, axis=1), jnp.concatenate(lower, axis=1)], axis=0
-        )
-        height = pad_ref.shape[0]
-        turned = pltpu.roll(pad_ref[...], lax.rem(height - dy, height), axis=0)
-        shifted = turned[:side].astype(jnp.bfloat16)
-        windows = jnp.concatenate(
+        return [jnp.concatenate(upper, axis=1), jnp.concatenate(lower, axis=1)]
+
+    def windows_of(ref, r):
+        shifted = ref[r : r + side, :].astype(jnp.bfloat16)
+        return jnp.concatenate(
             [shifted[:, t * side : (t + 2) * side] for t in range(tiles)], axis=0
         )
-        return jnp.dot(windows, band, preferred_element_type=jnp.float32)
-
-    acc[...] = product(0)
+
+    acc[...] = jnp.dot(
+        windows_of(pad_ref, 0),
+        jnp.concatenate(band_of(0), axis=0),
+        preferred_element_type=jnp.float32,
+    )
+    height = pad_ref.shape[0]
+    group = 4 if (kernel_side - 1) % 4 == 0 else 2
 
     def step(i, carry):
-        acc[...] += product(2 * i + 1) + product(2 * i + 2)
+        dy = group * i + 1
+        turned[...] = pltpu.roll(pad_ref[...], height - dy, axis=0)
+        windows = jnp.concatenate([windows_of(turned, r) for r in range(group)], axis=1)
+        band = jnp.concatenate([x for r in range(group) for x in band_of(dy + r)], axis=0)
+        acc[...] += jnp.dot(windows, band, preferred_element_type=jnp.float32)
         return carry
 
-    lax.fori_loop(0, (kernel_side - 1) // 2, step, 0)
+    lax.fori_loop(0, (kernel_side - 1) // group, step, 0)
 
     for t in range(tiles):
         planes = [
@@ -391,7 +398,10 @@
         out_shape=jax.ShapeDtypeStruct((visit_count, side, tiles * side), jnp.bfloat16),
         in_specs=[pl.BlockSpec(memory_space=pltpu.SMEM), vmem, vmem, vmem, vmem],
         out_specs=vmem,
-        scratch_shapes=[pltpu.VMEM((tiles * side, basis_count * side), jnp.float32)],
+        scratch_shapes=[
+            pltpu.VMEM((tiles * side, basis_count * side), jnp.float32),
+            pltpu.VMEM(padded.shape, jnp.float32),
+        ],
         compiler_params=pltpu.CompilerParams(vmem_limit_bytes=48 * 2**20),
     )(mixture.reshape(visit_count, tiles * basis_count), padded, rows, slab_tiles, valid)
 

time: 72.9 us -> 67.5 us (0.926)
  Pallas kernels: 59.8 us -> 54.4 us
    pallas_call x1, Pallas kernels: 20.2 us -> 14.8 us  [filter_and_subtract(): pl.pallas_call(functools.partial(difference_kernel, basis_count, kernel_s...]
where the time goes in v4:
time: 67.5 us; the launch traced here: 67.2 us
  Pallas kernels  54.4 us (81%)
  matrix products  6.23 us (9%)
  local copies, waits for them, and re-layouts  4.64 us (7%)
  other arithmetic  1.8 us (3%)
    pallas_call x1, Pallas kernels, padded_coadd(): pl.pallas_call(functools.partial(coadd_kernel, sizes, margin), out_shape=...  21 us
    pallas_call x1, Pallas kernels, exchange_tiles(): pl.pallas_call(exchange_kernel, out_shape=(jax.ShapeDtypeStruct(tiles, jn...  17.6 us
    pallas_call x1, Pallas kernels, filter_and_subtract(): pl.pallas_call(functools.partial(difference_kernel, basis_count, kernel_s...  14.8 us
    dot_general x1, matrix products, warp_tiles(): jnp.einsum('vtaq,vtbq->vtab', halfway, col_weights, preferred_element_typ...  5.17 us
    unnamed x18, local copies, waits for them, and re-layouts  3.85 us

profile of v4, /device:TPU:0, one launch (start us, length us, event | category | flops | bytes accessed | tf_op | source)
XLA Modules:
  0.0 67.2 jit_solution(9536787257038656260)
XLA Ops:
  0.0 0.8 %add_select_fusion.3 = (s32[2,8,32]{2,1,0:T(8,128)S(1)}, pred[2,8,32]{2,1,0:T(8,128)(4,1)S(1)}) fusion(s32[8,8,32]{2,1,0:T(8,128)} %param.15, s32[]{:T(128)S(6)} %select_n.91), kind=kLoop, calls=%fused_computation.161 | loop fusion | flops 7680 | bytes 4612 | tf_op jit(solution)/shard_map/jit(floor_divide)/jit(_where)/select_n | solution.py:17
  0.8 0.0 copy-done.1
  0.8 0.6 fusion.26.valid_ref
  1.5 0.7 copy-done.5
  2.2 0.1 and_select_fusion.1
  2.2 0.1 reshape.232
  2.3 0.2 convert_reduce_fusion
  2.5 0.1 add.129
  2.6 0.1 select_reduce_fusion.1
  2.7 0.1 convert_element_type.110
  2.8 0.7 %copy-done.6 = s32[2,8]{1,0:T(2,128)S(1)} copy-done((s32[2,8]{1,0:T(2,128)S(1)}, s32[2,8]{1,0:T(2,128)}, u32[]{:S(2)}) %copy-start.6) | copy-done | bytes 88
  3.5 0.1 fusion.134
  3.5 0.6 copy-done.8
  4.2 0.1 multiply_reduce_fusion.1
  4.2 0.6 copy-done.3
  4.9 0.1 broadcast_subtract_fusion
  5.0 5.2 %convolution_convert_fusion = bf16[2,8,128,128]{3,2,1,0:T(8,128)(2,1)S(1)} fusion(bf16[2,8,128,128]{3,2,1,0:T(8,128)(2,1)S(1)} %copy-done, f32[2,8]{1,0:T(2,128)S(1)} %bitcast.12, f32[2,8]{1,0:T(2,128)S(1)} %bitcast.11, f32[128,128]{1,0:T(8,128)S(1)} %broadcast_subtract_fusion), kind=kOutput, calls=%fused_computation.48 | convolution fusion | flops 172490752 | bytes 1114240 | tf_op jit(solution)/shard_map/vtaq,vtbq->vtab/dot_general | solution.py:40
  10.1 17.6 %shard_map.91 = (bf16[4,5,128,128]{3,2,1,0:T(8,128)(2,1)S(1)}, bf16[4,16,128]{2,1,0:T(8,128)(2,1)S(1)}) custom-call(s32[20]{0:T(128)S(1)} %get-tuple-element.19.source_ref, bf16[16,128,128]{2,1,0:T(8,128)(2,1)S(1)} %bitcast.9, bf16[4,16,128]{2,1,0:T(8,128)(2,1)S(1)} %pad.10.label_ref), custom_call_target="tpu_custom_call" | custom-call | tf_op jit(solution)/shard_map/pallas_call | solution.py:268
  27.7 0.1 reshape.236
  27.8 0.2 select_reduce_fusion.seat_ref
  28.0 1.0 %shard_map.92 = (bf16[2,8,128,128]{3,2,1,0:T(8,128)(2,1)S(1)}, bf16[8,128,128]{2,1,0:T(8,128)(2,1)S(1)}, bf16[8,128,128]{2,1,0:T(8,128)(2,1)S(1)}, bf16[8,128,128]{2,1,0:T(8,128)(2,1)S(1)}) custom-call(s32[16]{0:T(128)S(1)} %select_reduce_fusion.seat_ref, bf16[20,128,128]{2,1,0:T(8,128)(2,1)S(1)} %bitcast.8, bf16[2,8,128,128]{3,2,1,0:T(8,128)(2,1)S(1)} %fusion.26.valid_ref), custom_call_target="tpu_custom_call" | custom-call | tf_op jit(solution)/shard_map/pallas_call | solution.py:321
  29.0 0.1 broadcast_in_dim_reshape.2
  29.1 0.4 fusion.27.tally_ref
  29.6 21.0 %shard_map.93.pad_ref = f32[160,1152]{1,0:T(8,128)S(1)} custom-call(bf16[8,128,128]{2,1,0:T(8,128)(2,1)S(1)} %get-tuple-element.14.sum_ref, bf16[8,128,128]{2,1,0:T(8,128)(2,1)S(1)} %get-tuple-element.15.high_ref, bf16[8,128,128]{2,1,0:T(8,128)(2,1)S(1)} %get-tuple-element.16.low_ref, bf16[8,128,128]{2,1,0:T(8,128)(2,1)S(1)} %fusion.27.tally_ref), custom_call_target="tpu_custom_call" | custom-call | tf_op jit(solution)/shard_map/pallas_call | solution.py:194
  50.6 0.1 slice.27
  50.8 0.6 copy-done.7
  51.4 0.1 fusion.132
  51.5 0.6 copy-done.4
  52.1 0.1 multiply_reduce_fusion
  52.2 0.1 copy.17
  52.3 0.1 reshape.231.mix_ref
  52.4 14.8 %shard_map.94 = bf16[2,128,1024]{2,1,0:T(8,128)(2,1)} custom-call(f32[2,32]{1,0:T(2,128)S(1)} %reshape.231.mix_ref, f32[160,1152]{1,0:T(8,128)S(1)} %shard_map.93.pad_ref, f32[132,128]{1,0:T(8,128)S(1)} %reshape.235.row_ref, bf16[2,8,128,128]{3,2,1,0:T(8,128)(2,1)S(1)} %get-tuple-element.17.slab_ref, bf16[2,8,128,128]{3,2,1,0:T(8,128)(2,1)S(1)} %fusion.26.valid_ref), custom_call_target="tpu_custom_call" | custom-call | tf_op jit(solution)/shard_map/pallas_call | solution.py:396
  (26 shorter events, 0.2 us)
Async XLA Ops:
  0.0 4.9 %copy-start = (bf16[2,8,128,128]{3,2,1,0:T(8,128)(2,1)S(1)}, bf16[2,8,128,128]{3,2,1,0:T(8,128)(2,1)}, u32[]{:S(2)}) copy-start(bf16[2,8,128,128]{3,2,1,0:T(8,128)(2,1)} %param.10) | copy-start | bytes 1572868
  0.0 0.8 %copy-start.1 = (s32[8,8,32]{2,1,0:T(8,128)S(1)}, s32[8,8,32]{2,1,0:T(8,128)}, u32[]{:S(2)}) copy-start(s32[8,8,32]{2,1,0:T(8,128)} %param.15) | copy-start | bytes 24580
  1.5 0.7 %copy-start.5 = (s32[2,8]{1,0:T(2,128)S(1)}, s32[2,8]{1,0:T(2,128)}, u32[]{:S(2)}) copy-start(s32[2,8]{1,0:T(2,128)} %param.14) | copy-start | bytes 196
  2.8 0.7 %copy-start.6 = (s32[2,8]{1,0:T(2,128)S(1)}, s32[2,8]{1,0:T(2,128)}, u32[]{:S(2)}) copy-start(s32[2,8]{1,0:T(2,128)} %param.12) | copy-start | bytes 196
  3.5 0.7 %copy-start.8 = (f32[16,2]{0,1:T(2,128)S(1)}, f32[16,2]{0,1:T(2,128)}, u32[]{:S(2)}) copy-start(f32[16,2]{0,1:T(2,128)} %param.13) | copy-start | bytes 388
  4.2 0.7 %copy-start.3 = (s32[2,8,2]{1,2,0:T(2,128)S(1)}, s32[2,8,2]{1,2,0:T(2,128)}, u32[]{:S(2)}) copy-start(s32[2,8,2]{1,2,0:T(2,128)} %param.11) | copy-start | bytes 388
  29.5 21.0 %copy-start.2 = (bf16[4,33,33]{2,0,1:T(4,128)(2,1)S(1)}, bf16[4,33,33]{2,0,1:T(4,128)(2,1)}, u32[]{:S(2)}) copy-start(bf16[4,33,33]{2,0,1:T(4,128)(2,1)} %param.16) | copy-start | bytes 26140
  50.7 0.7 %copy-start.7 = (s32[2,8]{1,0:T(2,128)S(1)}, s32[2,8]{1,0:T(2,128)}, u32[]{:S(2)}) copy-start(s32[2,8]{1,0:T(2,128)} %param.17) | copy-start | bytes 196
  51.4 0.7 %copy-start.4 = (f32[16,4]{0,1:T(4,128)S(1)}, f32[16,4]{0,1:T(4,128)}, u32[]{:S(2)}) copy-start(f32[16,4]{0,1:T(4,128)} %param.18) | copy-start | bytes 772

commit v5 on v4

--- a/solution.py
+++ b/solution.py
@@ -356,7 +356,7 @@
         preferred_element_type=jnp.float32,
     )
     height = pad_ref.shape[0]
-    group = 4 if (kernel_side - 1) % 4 == 0 else 2
+    group = 8 if (kernel_side - 1) % 8 == 0 else 2
 
     def step(i, carry):
         dy = group * i + 1

time: 67.5 us -> 65.7 us (0.973)
  Pallas kernels: 54.4 us -> 52.6 us
    pallas_call x1, Pallas kernels: 14.8 us -> 13.1 us  [filter_and_subtract(): pl.pallas_call(functools.partial(difference_kernel, basis_count, kernel_s...]
where the time goes in v5:
time: 65.7 us; the launch traced here: 65.5 us
  Pallas kernels  52.6 us (80%)
  matrix products  6.23 us (9%)
  local copies, waits for them, and re-layouts  4.64 us (7%)
  other arithmetic  1.8 us (3%)
    pallas_call x1, Pallas kernels, padded_coadd(): pl.pallas_call(functools.partial(coadd_kernel, sizes, margin), out_shape=...  21 us
    pallas_call x1, Pallas kernels, exchange_tiles(): pl.pallas_call(exchange_kernel, out_shape=(jax.ShapeDtypeStruct(tiles, jn...  17.6 us
    pallas_call x1, Pallas kernels, filter_and_subtract(): pl.pallas_call(functools.partial(difference_kernel, basis_count, kernel_s...  13.1 us
    dot_general x1, matrix products, warp_tiles(): jnp.einsum('vtaq,vtbq->vtab', halfway, col_weights, preferred_element_typ...  5.17 us
    unnamed x18, local copies, waits for them, and re-layouts  3.85 us

profile of v5, /device:TPU:0, one launch (start us, length us, event | category | flops | bytes accessed | tf_op | source)
XLA Modules:
  0.0 65.5 jit_solution(3721895506464978416)
XLA Ops:
  0.0 0.8 %add_select_fusion.3 = (s32[2,8,32]{2,1,0:T(8,128)S(1)}, pred[2,8,32]{2,1,0:T(8,128)(4,1)S(1)}) fusion(s32[8,8,32]{2,1,0:T(8,128)} %param.15, s32[]{:T(128)S(6)} %select_n.91), kind=kLoop, calls=%fused_computation.161 | loop fusion | flops 7680 | bytes 4612 | tf_op jit(solution)/shard_map/jit(floor_divide)/jit(_where)/select_n | solution.py:17
  0.8 0.0 copy-done.1
  0.8 0.6 fusion.26.valid_ref
  1.5 0.7 %copy-done.5 = s32[2,8]{1,0:T(2,128)S(1)} copy-done((s32[2,8]{1,0:T(2,128)S(1)}, s32[2,8]{1,0:T(2,128)}, u32[]{:S(2)}) %copy-start.5) | copy-done | bytes 88
  2.2 0.1 and_select_fusion.1
  2.2 0.1 reshape.232
  2.3 0.2 convert_reduce_fusion
  2.5 0.1 add.129
  2.6 0.1 select_reduce_fusion.1
  2.7 0.1 convert_element_type.110
  2.8 0.7 %copy-done.6 = s32[2,8]{1,0:T(2,128)S(1)} copy-done((s32[2,8]{1,0:T(2,128)S(1)}, s32[2,8]{1,0:T(2,128)}, u32[]{:S(2)}) %copy-start.6) | copy-done | bytes 88
  3.5 0.1 fusion.134
  3.5 0.6 copy-done.8
  4.2 0.1 multiply_reduce_fusion.1
  4.2 0.6 copy-done.3
  4.9 0.1 broadcast_subtract_fusion
  5.0 5.2 %convolution_convert_fusion = bf16[2,8,128,128]{3,2,1,0:T(8,128)(2,1)S(1)} fusion(bf16[2,8,128,128]{3,2,1,0:T(8,128)(2,1)S(1)} %copy-done, f32[2,8]{1,0:T(2,128)S(1)} %bitcast.12, f32[2,8]{1,0:T(2,128)S(1)} %bitcast.11, f32[128,128]{1,0:T(8,128)S(1)} %broadcast_subtract_fusion), kind=kOutput, calls=%fused_computation.48 | convolution fusion | flops 172490752 | bytes 1114240 | tf_op jit(solution)/shard_map/vtaq,vtbq->vtab/dot_general | solution.py:40
  10.1 17.6 %shard_map.91 = (bf16[4,5,128,128]{3,2,1,0:T(8,128)(2,1)S(1)}, bf16[4,16,128]{2,1,0:T(8,128)(2,1)S(1)}) custom-call(s32[20]{0:T(128)S(1)} %get-tuple-element.19.source_ref, bf16[16,128,128]{2,1,0:T(8,128)(2,1)S(1)} %bitcast.9, bf16[4,16,128]{2,1,0:T(8,128)(2,1)S(1)} %pad.10.label_ref), custom_call_target="tpu_custom_call" | custom-call | tf_op jit(solution)/shard_map/pallas_call | solution.py:268
  27.7 0.1 reshape.236
  27.8 0.2 select_reduce_fusion.seat_ref
  28.0 1.0 %shard_map.92 = (bf16[2,8,128,128]{3,2,1,0:T(8,128)(2,1)S(1)}, bf16[8,128,128]{2,1,0:T(8,128)(2,1)S(1)}, bf16[8,128,128]{2,1,0:T(8,128)(2,1)S(1)}, bf16[8,128,128]{2,1,0:T(8,128)(2,1)S(1)}) custom-call(s32[16]{0:T(128)S(1)} %select_reduce_fusion.seat_ref, bf16[20,128,128]{2,1,0:T(8,128)(2,1)S(1)} %bitcast.8, bf16[2,8,128,128]{3,2,1,0:T(8,128)(2,1)S(1)} %fusion.26.valid_ref), custom_call_target="tpu_custom_call" | custom-call | tf_op jit(solution)/shard_map/pallas_call | solution.py:321
  29.0 0.1 broadcast_in_dim_reshape.2
  29.1 0.4 fusion.27.tally_ref
  29.6 21.0 %shard_map.93.pad_ref = f32[160,1152]{1,0:T(8,128)S(1)} custom-call(bf16[8,128,128]{2,1,0:T(8,128)(2,1)S(1)} %get-tuple-element.14.sum_ref, bf16[8,128,128]{2,1,0:T(8,128)(2,1)S(1)} %get-tuple-element.15.high_ref, bf16[8,128,128]{2,1,0:T(8,128)(2,1)S(1)} %get-tuple-element.16.low_ref, bf16[8,128,128]{2,1,0:T(8,128)(2,1)S(1)} %fusion.27.tally_ref), custom_call_target="tpu_custom_call" | custom-call | tf_op jit(solution)/shard_map/pallas_call | solution.py:194
  50.6 0.1 slice.27
  50.8 0.6 copy-done.7
  51.4 0.1 fusion.132
  51.5 0.6 copy-done.4
  52.1 0.1 multiply_reduce_fusion
  52.2 0.1 copy.17
  52.3 0.1 reshape.231.mix_ref
  52.4 13.1 %shard_map.94 = bf16[2,128,1024]{2,1,0:T(8,128)(2,1)} custom-call(f32[2,32]{1,0:T(2,128)S(1)} %reshape.231.mix_ref, f32[160,1152]{1,0:T(8,128)S(1)} %shard_map.93.pad_ref, f32[132,128]{1,0:T(8,128)S(1)} %reshape.235.row_ref, bf16[2,8,128,128]{3,2,1,0:T(8,128)(2,1)S(1)} %get-tuple-element.17.slab_ref, bf16[2,8,128,128]{3,2,1,0:T(8,128)(2,1)S(1)} %fusion.26.valid_ref), custom_call_target="tpu_custom_call" | custom-call | tf_op jit(solution)/shard_map/pallas_call | solution.py:396
  (26 shorter events, 0.2 us)
Async XLA Ops:
  0.0 4.9 %copy-start = (bf16[2,8,128,128]{3,2,1,0:T(8,128)(2,1)S(1)}, bf16[2,8,128,128]{3,2,1,0:T(8,128)(2,1)}, u32[]{:S(2)}) copy-start(bf16[2,8,128,128]{3,2,1,0:T(8,128)(2,1)} %param.10) | copy-start | bytes 1572868
  0.0 0.8 %copy-start.1 = (s32[8,8,32]{2,1,0:T(8,128)S(1)}, s32[8,8,32]{2,1,0:T(8,128)}, u32[]{:S(2)}) copy-start(s32[8,8,32]{2,1,0:T(8,128)} %param.15) | copy-start | bytes 24580
  1.5 0.7 %copy-start.5 = (s32[2,8]{1,0:T(2,128)S(1)}, s32[2,8]{1,0:T(2,128)}, u32[]{:S(2)}) copy-start(s32[2,8]{1,0:T(2,128)} %param.14) | copy-start | bytes 196
  2.8 0.7 %copy-start.6 = (s32[2,8]{1,0:T(2,128)S(1)}, s32[2,8]{1,0:T(2,128)}, u32[]{:S(2)}) copy-start(s32[2,8]{1,0:T(2,128)} %param.12) | copy-start | bytes 196
  3.5 0.7 %copy-start.8 = (f32[16,2]{0,1:T(2,128)S(1)}, f32[16,2]{0,1:T(2,128)}, u32[]{:S(2)}) copy-start(f32[16,2]{0,1:T(2,128)} %param.13) | copy-start | bytes 388
  4.2 0.7 %copy-start.3 = (s32[2,8,2]{1,2,0:T(2,128)S(1)}, s32[2,8,2]{1,2,0:T(2,128)}, u32[]{:S(2)}) copy-start(s32[2,8,2]{1,2,0:T(2,128)} %param.11) | copy-start | bytes 388
  29.5 21.0 %copy-start.2 = (bf16[4,33,33]{2,0,1:T(4,128)(2,1)S(1)}, bf16[4,33,33]{2,0,1:T(4,128)(2,1)}, u32[]{:S(2)}) copy-start(bf16[4,33,33]{2,0,1:T(4,128)(2,1)} %param.16) | copy-start | bytes 26140
  50.7 0.7 %copy-start.7 = (s32[2,8]{1,0:T(2,128)S(1)}, s32[2,8]{1,0:T(2,128)}, u32[]{:S(2)}) copy-start(s32[2,8]{1,0:T(2,128)} %param.17) | copy-start | bytes 196
  51.4 0.7 %copy-start.4 = (f32[16,4]{0,1:T(4,128)S(1)}, f32[16,4]{0,1:T(4,128)}, u32[]{:S(2)}) copy-start(f32[16,4]{0,1:T(4,128)} %param.18) | copy-start | bytes 772
